TPU v7x, 32 devices: a whole 2x2x4 slice. The times are simulated.
32 devices in a mesh: req: 8 (over z, x), mlp: 4 (over y, core).
Axes of the slice: x: 2, y: 2, z: 4, core: 2. Of those that a mesh axis runs over, the one named last changes fastest.
Arguments:
- tokens: bfloat16 [16384, 1024], P(('req', 'mlp')), may hold values from -72 to 72
- attend_weight: bfloat16 [1024, 3072], replicated, may hold values from -0.1875 to 0.1875
- output_weight: bfloat16 [1024, 1024], replicated, may hold values from -0.1875 to 0.1875
- attend_gain: float32 [1024], replicated, may hold values from 0.1 to 1.9
- up_weight: bfloat16 [1024, 4096], P(None, 'mlp'), may hold values from -0.1875 to 0.1875
- down_weight: bfloat16 [1024, 4096], P(None, 'mlp'), may hold values from -0.09375 to 0.09375
- mlp_gain: float32 [1024], replicated, may hold values from 0.1 to 1.9
- embed_weight: bfloat16 [1024, 128], replicated, may hold values from -0.1875 to 0.1875
- query_length: int32 [128], P(('req', 'mlp')), may hold values from 1 to 128, 12288 in all
- documents: bfloat16 [64, 256, 128], P('req', 'mlp'), may hold values from -0.54 to 0.54
- document_length: int32 [64], P('req'), may hold values from 1 to 256, 8256 in all
- candidates: int32 [128, 8], P(('req', 'mlp')), may hold values from 0 to 63
Outputs:
- embedded: bfloat16 [16384, 128], P(('req', 'mlp'))
- scores: float32 [128, 8], P(('req', 'mlp'))
All inputs are finite; a program needn't handle non-finite values. No bound on the sum of `query_length` or of `document_length` on one device may be relied on, other than what follows from the above.
Results may differ from a plain program's by a relative error of at most 0.015.
The roundings to bfloat16 on the way count: a program that leaves them out, or rounds other values in their place, can miss the bound.
Values may be sent and summed in bfloat16 or wider, within the bound.
A program may use at most 128 MiB of HBM per device.

v0:
```python
import jax
import jax.numpy as jnp
from jax import lax
from jax.sharding import PartitionSpec as P

D = 1024
HEADS = 16
HD = 64
P_SIZE = 128
SEQ = 128


def norm_rows(values, scaling):
    average = jnp.mean(values, axis=-1, keepdims=True)
    centred = values - average
    variance = jnp.mean(centred * centred, axis=-1, keepdims=True)
    return centred * lax.rsqrt(variance + 1e-05) * scaling


def best_match(piece, flat_docs, live_doc):
    sims = lax.dot_general(
        piece, flat_docs, (((1,), (1,)), ((), ())), preferred_element_type=jnp.float32
    )
    sims = sims.reshape(piece.shape[0], live_doc.shape[0], live_doc.shape[1])
    sims = jnp.where(live_doc[None], sims, -1e30)
    return jnp.max(sims, axis=2)


def on_device(
    tokens,
    attend_weight,
    output_weight,
    attend_gain,
    up_weight,
    down_weight,
    mlp_gain,
    embed_weight,
    query_length,
    documents,
    document_length,
    candidates,
):
    rows = tokens.shape[0]
    requests = query_length.shape[0]
    held_docs = documents.shape[0]
    packed = jnp.dot(tokens, attend_weight, preferred_element_type=jnp.float32).astype(jnp.bfloat16)
    packed = packed.reshape(requests, SEQ, 3, HEADS, HD)
    live_slot = jnp.arange(SEQ)[None, :] < query_length[:, None]
    logits = jnp.einsum(
        "rqhd,rkhd->rhqk", packed[:, :, 0], packed[:, :, 1], preferred_element_type=jnp.float32
    ) * HD ** (-0.5)
    logits = jnp.where(live_slot[:, None, None, :], logits, -1e30)
    highest = jnp.max(logits, axis=-1, keepdims=True)
    weights = jnp.exp(logits - highest)
    probs = (weights / jnp.sum(weights, axis=-1, keepdims=True)).astype(jnp.bfloat16)
    context = jnp.einsum(
        "rhqk,rkhd->rqhd", probs, packed[:, :, 2], preferred_element_type=jnp.float32
    )
    context = context.astype(jnp.bfloat16).reshape(rows, D)
    attended = jnp.dot(context, output_weight, preferred_element_type=jnp.float32)
    normed = norm_rows(tokens.astype(jnp.float32) + attended, attend_gain).astype(jnp.bfloat16)
    hidden = jax.nn.gelu(
        jnp.dot(
            normed,
            lax.all_gather(up_weight, "mlp", axis=1, tiled=True),
            preferred_element_type=jnp.float32,
        ),
        approximate=False,
    ).astype(jnp.bfloat16)
    reduced = lax.dot_general(
        hidden,
        lax.all_gather(down_weight, "mlp", axis=1, tiled=True),
        (((1,), (1,)), ((), ())),
        preferred_element_type=jnp.float32,
    )
    layer_out = norm_rows(normed.astype(jnp.float32) + reduced, mlp_gain).astype(jnp.bfloat16)
    projected = jnp.dot(layer_out, embed_weight, preferred_element_type=jnp.float32)
    unit = projected * lax.rsqrt(jnp.sum(projected * projected, axis=-1, keepdims=True) + 1e-06)
    embedded = jnp.where(live_slot.reshape(rows, 1), unit, 0.0).astype(jnp.bfloat16)
    shard_rows = documents.shape[1]
    positions = lax.axis_index("mlp") * shard_rows + jnp.arange(shard_rows)
    live_doc = positions[None, :] < document_length[:, None]
    flat_docs = documents.reshape(held_docs * shard_rows, P_SIZE)
    partial_best = best_match(
        lax.all_gather(embedded, ("req", "mlp"), axis=0, tiled=True), flat_docs, live_doc
    )
    best = lax.pmax(partial_best.astype(jnp.bfloat16), "mlp").astype(partial_best.dtype)
    totals = jnp.sum(best.reshape(best.shape[0] // SEQ, SEQ, held_docs), axis=1)
    swapped = lax.all_to_all(totals, "req", split_axis=0, concat_axis=1, tiled=True)
    swapped = lax.dynamic_slice_in_dim(swapped, lax.axis_index("mlp") * requests, requests, 0)
    all_docs = swapped.shape[1]
    matches = candidates[:, :, None] == jnp.arange(all_docs, dtype=jnp.int32)[None, None, :]
    scores = jnp.sum(jnp.where(matches, swapped[:, None, :], 0.0), axis=2)
    return (embedded, scores)


def solution(mesh):
    return jax.shard_map(
        on_device,
        mesh=mesh,
        in_specs=(
            P(("req", "mlp"), None),
            P(),
            P(),
            P(),
            P(None, "mlp"),
            P(None, "mlp"),
            P(),
            P(),
            P(("req", "mlp")),
            P("req", "mlp", None),
            P("req"),
            P(("req", "mlp"), None),
        ),
        out_specs=(P(("req", "mlp"), None), P(("req", "mlp"), None)),
        check_vma=False,
    )
```

profile of v0, /device:TPU:0, one launch (start us, length us, event | category | flops | bytes accessed | tf_op | source)
XLA Modules:
  0.0 289.7 jit_solution(10713538578170630424)
XLA Ops:
  8.0 0.7 all-gather.6.cloned.1.call-update
  8.7 8.2 %convolution_convert_fusion = bf16[512,3072]{1,0:T(8,128)(2,1)} fusion(bf16[512,1024]{1,0:T(8,128)(2,1)} %param.12, bf16[1024,3072]{1,0:T(8,128)(2,1)} %param.13), kind=kOutput, calls=%fused_computation.21 | convolution fusion | flops 3222798336 | bytes 10485760 | tf_op jit(solution)/shard_map/dot_general | solution.py:46
  17.0 8.9 %reshape.125 = bf16[4,128,3,16,64]{4,3,2,1,0:T(8,128)(2,1)} reshape(bf16[512,3072]{1,0:T(8,128)(2,1)} %convolution_convert_fusion) | data formatting | bytes 6291456 | tf_op jit(solution)/shard_map/reshape | solution.py:47
  25.9 6.1 %fusion.67 = (bf16[4,128,1,16,64]{4,3,2,1,0:T(8,128)(2,1)}, bf16[4,128,1,16,64]{4,3,2,1,0:T(8,128)(2,1)}, bf16[4,128,1,16,64]{4,3,2,1,0:T(8,128)(2,1)}) fusion(bf16[4,128,3,16,64]{4,3,2,1,0:T(8,128)(2,1)} %reshape.125), kind=kLoop, calls=%fused_computation.99 | loop fusion | bytes 6291456 | tf_op jit(solution)/shard_map/slice | solution.py:57
  32.0 2.8 copy.70
  34.8 3.5 %copy.71 = bf16[4,128,1,16,64]{1,4,3,0,2:T(8,128)(2,1)} copy(bf16[4,128,1,16,64]{4,3,2,1,0:T(8,128)(2,1)} %get-tuple-element.14) | data formatting | bytes 2097152
  38.4 3.6 %copy.69 = bf16[4,128,1,16,64]{1,4,3,0,2:T(8,128)(2,1)} copy(bf16[4,128,1,16,64]{4,3,2,1,0:T(8,128)(2,1)} %get-tuple-element.12) | data formatting | bytes 2097152
  42.0 2.1 fusion.26
  44.1 1.7 fusion.68
  45.8 0.7 fusion.22
  46.5 0.9 copy.56
  47.4 1.4 fusion.69
  48.8 1.3 copy-done.2
  50.6 20.0 %all-gather.4.cloned.1.call-done = bf16[1024,4096]{1,0:T(8,128)(2,1)} async-done(((bf16[1024,1024]{1,0:T(8,128)(2,1)}), bf16[1024,4096]{1,0:T(8,128)(2,1)}) %all-gather.4.cloned.1.call-update) | async-done | bytes 8388624 | tf_op jit(solution)/shard_map/all_gather | solution.py:65
  70.6 59.9 %all-gather.6.cloned.1.call-done = bf16[1024,4096]{1,0:T(8,128)(2,1)} async-done(((bf16[1024,1024]{1,0:T(8,128)(2,1)}), bf16[1024,4096]{1,0:T(8,128)(2,1)}) %all-gather.6.cloned.1.call-update) | async-done | bytes 8388624 | tf_op jit(solution)/shard_map/all_gather | solution.py:72
  130.5 32.1 %fusion.70 = (f32[512]{0:T(512)S(1)}, f32[512,1024]{1,0:T(8,128)S(1)}) fusion(bf16[1024,4096]{1,0:T(8,128)(2,1)} %all-gather.6.cloned.1.call-done, f32[1024]{0:T(1024)S(1)} %copy-done.11, f32[512]{0:T(512)S(1)} %add_rsqrt_fusion.2, f32[512,1024]{1,0:T(8,128)} %copy-done.2, f32[512]{0:T(512)S(1)} %broadcast_multiply_fusion.1, ...), kind=kOutput, calls=%fused_computation.102 | convolution fusion | flops 8732016640 | bytes 20981760 | tf_op jit(solution)/shard_map/dot_general | solution.py:70
  164.5 64.0 %all-gather.8.cloned.1.call-done = bf16[16384,128]{0,1:T(8,128)(2,1)} async-done(((bf16[512,128]{0,1:T(8,128)(2,1)}), bf16[16384,128]{0,1:T(8,128)(2,1)}) %all-gather.8.cloned.1.call-update) | async-done | bytes 4194320 | tf_op jit(solution)/shard_map/all_gather | solution.py:85
  228.6 8.1 %select_reduce_fusion = bf16[16384,8]{0,1:T(8,128)(2,1)} fusion(bf16[8,64,128]{2,1,0:T(8,128)(2,1)S(1)} %copy-done.10, pred[8,64]{1,0:T(8,128)(4,1)S(1)} %broadcast_compare_fusion, bf16[16384,128]{0,1:T(8,128)(2,1)} %all-gather.8.cloned.1.call-done), kind=kOutput, calls=%fused_computation.1 | convolution fusion | flops 2164129792 | bytes 4588032 | tf_op jit(solution)/shard_map/dot_general | solution.py:21
  236.6 30.5 %all-reduce.2.cloned.1.call-done = bf16[128,128,8]{1,2,0:T(8,128)(2,1)} async-done(((bf16[128,128,8]{1,2,0:T(8,128)(2,1)}), bf16[128,128,8]{1,2,0:T(8,128)(2,1)}) %all-reduce.2.cloned.1.call-update) | async-done | bytes 262160 | tf_op jit(solution)/shard_map/pmax | solution.py:87
  267.1 1.2 convert_reduce_fusion
  269.1 5.5 %all-to-all-start = ((f32[8,1,128]{2,1,0:T(1,128)}), f32[8,1,128]{2,1,0:T(1,128)S(1)}, u32[]{:S(2)}, u32[]{:S(2)}) async-start(f32[8,1,128]{2,1,0:T(1,128)} %reshape.127), calls=%async_computation | async-start | bytes 8192 | tf_op jit(solution)/shard_map/all_to_all | solution.py:89
  274.6 0.8 copy.61
  275.3 5.7 %all-to-all-done = f32[8,1,128]{2,1,0:T(1,128)S(1)} async-done(((f32[8,1,128]{2,1,0:T(1,128)}), f32[8,1,128]{2,1,0:T(1,128)S(1)}, u32[]{:S(2)}, u32[]{:S(2)}) %all-to-all-start) | async-done | bytes 4128 | tf_op jit(solution)/shard_map/all_to_all | solution.py:89
  282.4 0.8 select_reduce_fusion.1
  (52 shorter events, 5.3 us)
Async XLA Ops:
  7.2 40.2 %copy-start = (bf16[1024,1024]{1,0:T(8,128)(2,1)S(1)}, bf16[1024,1024]{1,0:T(8,128)(2,1)}, u32[]{:S(2)}) copy-start(bf16[1024,1024]{1,0:T(8,128)(2,1)} %param.14) | copy-start | bytes 6291460
  7.2 63.4 %all-gather.4.cloned.1.call-start = ((), (), s32[]{:S(2)}) async-start(), calls=%async_computation.1 | async-start | bytes 10485760 | tf_op jit(solution)/shard_map/all_gather | solution.py:65
  7.9 122.6 %all-gather.6.cloned.1.call-start = ((), (), s32[]{:S(2)}) async-start(), calls=%async_computation.2 | async-start | bytes 10485760 | tf_op jit(solution)/shard_map/all_gather | solution.py:72
  8.7 219.9 %all-gather.8.cloned.1.call-start = ((), (), s32[]{:S(2)}) async-start(), calls=%async_computation.3 | async-start | bytes 4325376 | tf_op jit(solution)/shard_map/all_gather | solution.py:85
  25.9 16.0 %copy-start.12 = (s32[4]{0:T(128)S(1)}, s32[4]{0:T(128)}, u32[]{:S(2)}) copy-start(s32[4]{0:T(128)} %param.20) | copy-start | bytes 52
  41.9 3.8 %copy-start.4 = (bf16[4,128,1,16,64]{1,4,3,0,2:T(8,128)(2,1)S(1)}, bf16[4,128,1,16,64]{1,4,3,0,2:T(8,128)(2,1)}, u32[]{:S(2)}) copy-start(bf16[4,128,1,16,64]{1,4,3,0,2:T(8,128)(2,1)} %copy.69) | copy-start | bytes 3145732
  45.8 1.7 copy-start.5
  46.5 84.0 %copy-start.11 = (f32[1024]{0:T(1024)S(1)}, f32[1024]{0:T(1024)}, u32[]{:S(2)}) copy-start(f32[1024]{0:T(1024)} %param.15) | copy-start | bytes 12292
  48.8 1.4 copy-start.2
  50.5 112.5 %copy-start.6 = (bf16[1024,128]{1,0:T(8,128)(2,1)S(1)}, bf16[1024,128]{1,0:T(8,128)(2,1)}, u32[]{:S(2)}) copy-start(bf16[1024,128]{1,0:T(8,128)(2,1)} %param.19) | copy-start | bytes 786436
  50.5 112.5 %copy-start.7 = (f32[1024]{0:T(1024)S(1)}, f32[1024]{0:T(1024)}, u32[]{:S(2)}) copy-start(f32[1024]{0:T(1024)} %param.18) | copy-start | bytes 12292
  50.5 113.9 %copy-start.9 = (s32[8]{0:T(128)S(1)}, s32[8]{0:T(128)}, u32[]{:S(2)}) copy-start(s32[8]{0:T(128)} %param.22) | copy-start | bytes 100
  50.5 178.0 %copy-start.10 = (bf16[8,64,128]{2,1,0:T(8,128)(2,1)S(1)}, bf16[8,64,128]{2,1,0:T(8,128)(2,1)}, u32[]{:S(2)}) copy-start(bf16[8,64,128]{2,1,0:T(8,128)(2,1)} %param.21) | copy-start | bytes 393220
  164.4 102.8 %all-reduce.2.cloned.1.call-start = ((), (), s32[]{:S(2)}) async-start(), calls=%async_computation.4 | async-start | bytes 524288 | tf_op jit(solution)/shard_map/pmax | solution.py:87
  164.4 118.7 %copy-start.1 = (bf16[1024,1024]{1,0:T(8,128)(2,1)S(1)}, bf16[1024,1024]{1,0:T(8,128)(2,1)}, u32[]{:S(2)}) copy-start(bf16[1024,1024]{1,0:T(8,128)(2,1)} %param.14) | copy-start | bytes 6291460
  164.5 110.0 %copy-start.3 = (bf16[512,128]{0,1:T(8,128)(2,1)S(1)}, bf16[512,128]{0,1:T(8,128)(2,1)}, u32[]{:S(2)}) copy-start(bf16[512,128]{0,1:T(8,128)(2,1)} %select_convert_fusion) | copy-start | bytes 393220
  164.5 117.9 %copy-start.8 = (s32[4,8]{1,0:T(4,128)S(1)}, s32[4,8]{1,0:T(4,128)}, u32[]{:S(2)}) copy-start(s32[4,8]{1,0:T(4,128)} %param.23) | copy-start | bytes 388
  269.1 12.0 %all-to-all-start = ((f32[8,1,128]{2,1,0:T(1,128)}), f32[8,1,128]{2,1,0:T(1,128)S(1)}, u32[]{:S(2)}, u32[]{:S(2)}) async-start(f32[8,1,128]{2,1,0:T(1,128)} %reshape.127), calls=%async_computation | async-start | bytes 8192 | tf_op jit(solution)/shard_map/all_to_all | solution.py:89
Sparse Core Ops, SparseCore 0:
  9.6 60.9 all-gather.3
  72.2 58.2 all-gather.5
  164.5 64.0 all-gather.7
  236.8 30.3 all-reduce.1
where the time goes:
time: 290 us
  waiting for transfers between devices  182 us (63%)
  matrix products  53.2 us (18%)
  local copies, waits for them, and re-layouts  29.5 us (10%)
  between operations  14 us (5%)
  other arithmetic  5.8 us (2%)
  starting transfers between devices  5.67 us (2%)
    all_gather x1, waiting for transfers between devices, on_device(): lax.all_gather(embedded, ('req', 'mlp'), axis=0, tiled=True)  64 us
    all_gather x1, waiting for transfers between devices, on_device(): lax.all_gather(down_weight, 'mlp', axis=1, tiled=True)  59.9 us
    dot_general x1, matrix products, on_device(): lax.dot_general(hidden, lax.all_gather(down_weight, 'mlp', axis=1, tiled=...  32.1 us
    pmax x1, waiting for transfers between devices, on_device(): lax.pmax(partial_best.astype(jnp.bfloat16), 'mlp')  30.5 us
    all_gather x1, waiting for transfers between devices, on_device(): lax.all_gather(up_weight, 'mlp', axis=1, tiled=True)  20 us
    unnamed x32, local copies, waits for them, and re-layouts  12.9 us
    reshape x1, local copies, waits for them, and re-layouts, on_device(): packed = packed.reshape(requests, SEQ, 3, HEADS, HD)  8.91 us
    dot_general x1, matrix products, on_device(): jnp.dot(tokens, attend_weight, preferred_element_type=jnp.float32)  8.24 us
  transfers between devices with their start and end apart: 5, of which 5 were waited for; matrix products, arithmetic and copies ran while one was open for 14% of the time, Pallas kernels for 0%

commit v1 on v0

v1 whole, which is shorter than its diff:
```python
import functools

import jax
import jax.numpy as jnp
from jax import lax
from jax.experimental import pallas as pl
from jax.experimental.pallas import tpu as pltpu
from jax.sharding import PartitionSpec as P

D = 1024
HEADS = 16
HD = 64
P_SIZE = 128
SEQ = 128
CORES = 2
DEPTH = 4
MIB = 1024 * 1024


def norm_rows(values, scaling):
    average = jnp.mean(values, axis=-1, keepdims=True)
    centred = values - average
    variance = jnp.mean(centred * centred, axis=-1, keepdims=True)
    return centred * lax.rsqrt(variance + 1e-05) * scaling


def attend_kernel(length_ref, tokens_ref, attend_ref, output_ref, gain_ref, normed_ref, packed, context):
    rows = tokens_ref.shape[0]
    wide = 512

    def project(step, carry):
        columns = pl.ds(pl.multiple_of(step * wide, wide), wide)
        packed[:, columns] = jnp.dot(
            tokens_ref[...], attend_ref[:, columns], preferred_element_type=jnp.float32
        ).astype(jnp.bfloat16)
        return carry

    lax.fori_loop(0, 3 * D // wide, project, 0)
    lane = lax.broadcasted_iota(jnp.int32, (SEQ, 2 * HD), 1)
    low = lane < HD
    key_slot = lax.broadcasted_iota(jnp.int32, (2 * SEQ, SEQ), 1)

    def one_request(request, carry):
        here = pl.ds(pl.multiple_of(request * SEQ, SEQ), SEQ)
        live = key_slot < length_ref[request]
        for pair in range(HEADS // 2):
            at = pair * 2 * HD
            query = packed[here, at : at + 2 * HD]
            keys = packed[here, D + at : D + at + 2 * HD]
            value = packed[here, 2 * D + at : 2 * D + at + 2 * HD]
            none = jnp.zeros_like(query)
            both = jnp.concatenate([jnp.where(low, query, none), jnp.where(low, none, query)], axis=0)
            logits = lax.dot_general(
                both, keys, (((1,), (1,)), ((), ())), preferred_element_type=jnp.float32
            ) * HD ** (-0.5)
            logits = jnp.where(live, logits, -1e30)
            weights = jnp.exp(logits - jnp.max(logits, axis=-1, keepdims=True))
            probs = (weights / jnp.sum(weights, axis=-1, keepdims=True)).astype(jnp.bfloat16)
            mixed = jnp.dot(probs, value, preferred_element_type=jnp.float32)
            context[here, at : at + 2 * HD] = jnp.where(low, mixed[:SEQ], mixed[SEQ:]).astype(jnp.bfloat16)
        return carry

    lax.fori_loop(0, rows // SEQ, one_request, 0)

    def finish(step, carry):
        here = pl.ds(pl.multiple_of(step * SEQ, SEQ), SEQ)
        attended = jnp.dot(context[here, :], output_ref[...], preferred_element_type=jnp.float32)
        normed_ref[here, :] = norm_rows(
            tokens_ref[here, :].astype(jnp.float32) + attended, gain_ref[...]
        ).astype(jnp.bfloat16)
        return carry

    lax.fori_loop(0, rows // SEQ, finish, 0)


def attend(tokens, attend_weight, output_weight, attend_gain, query_length):
    rows = tokens.shape[0]
    vmem = pl.BlockSpec(memory_space=pltpu.VMEM)
    return pl.pallas_call(
        attend_kernel,
        out_shape=jax.ShapeDtypeStruct((rows, D), jnp.bfloat16),
        in_specs=[pl.BlockSpec(memory_space=pltpu.SMEM), vmem, vmem, vmem, vmem],
        out_specs=vmem,
        scratch_shapes=[pltpu.VMEM((rows, 3 * D), jnp.bfloat16), pltpu.VMEM((rows, D), jnp.bfloat16)],
        compiler_params=pltpu.CompilerParams(vmem_limit_bytes=32 * MIB),
        cost_estimate=pl.CostEstimate(flops=rows * D * D * 9, bytes_accessed=10 * MIB, transcendentals=rows * SEQ * HEADS),
        name="attend",
    )(query_length, tokens, attend_weight, output_weight, attend_gain.reshape(1, D))


def score_kernel(spots_ref, limits_ref, embedded_ref, pieces_ref, best_ref):
    requests, picks, parts = spots_ref.shape
    piece_rows = pieces_ref.shape[1]
    position = lax.broadcasted_iota(jnp.int32, (parts * piece_rows, SEQ), 0)

    def one_request(request, carry):
        block = embedded_ref[pl.ds(pl.multiple_of(request * SEQ, SEQ), SEQ), :]
        found = []
        for pick in range(picks):
            chosen = jnp.concatenate([pieces_ref[spots_ref[request, pick, part]] for part in range(parts)], axis=0)
            sims = lax.dot_general(
                chosen, block, (((1,), (1,)), ((), ())), preferred_element_type=jnp.float32
            )
            sims = jnp.where(position < limits_ref[request, pick], sims, -1e30)
            found.append(jnp.max(sims, axis=0, keepdims=True))
        best_ref[request] = jnp.concatenate(found, axis=0)
        return carry

    lax.fori_loop(0, requests, one_request, 0)


def score(embedded, pieces, spots, limits):
    requests, picks, parts = spots.shape
    smem, vmem = pl.BlockSpec(memory_space=pltpu.SMEM), pl.BlockSpec(memory_space=pltpu.VMEM)
    best = pl.pallas_call(
        score_kernel,
        out_shape=jax.ShapeDtypeStruct((requests, picks, SEQ), jnp.float32),
        in_specs=[smem, smem, vmem, vmem],
        out_specs=vmem,
        compiler_params=pltpu.CompilerParams(vmem_limit_bytes=32 * MIB),
        cost_estimate=pl.CostEstimate(flops=2 * requests * picks * 256 * SEQ * P_SIZE, bytes_accessed=5 * MIB, transcendentals=0),
        name="score",
    )(spots, limits, embedded, pieces)
    return jnp.sum(best, axis=2)


def on_device(
    req_size,
    mlp_size,
    tokens,
    attend_weight,
    output_weight,
    attend_gain,
    up_weight,
    down_weight,
    mlp_gain,
    embed_weight,
    query_length,
    documents,
    document_length,
    candidates,
):
    rows = tokens.shape[0]
    held_docs, shard_rows = documents.shape[:2]
    width, tall = req_size // DEPTH, mlp_size // CORES
    req, mlp = lax.axis_index("req"), lax.axis_index("mlp")
    z, x, y, core = req // width, req % width, mlp // CORES, mlp % CORES

    def to_core(block):
        return lax.ppermute(block, "mlp", [(m, m ^ 1) for m in range(mlp_size)])

    def along_y(block, hops):
        return lax.ppermute(block, "mlp", [(m, (m + CORES * hops) % mlp_size) for m in range(mlp_size)])

    def along_x(block, hops):
        return lax.ppermute(
            block, "req", [(r, r // width * width + (r % width + hops) % width) for r in range(req_size)]
        )

    def to_pair(block, stride):
        return lax.ppermute(block, "req", [(r, r ^ stride) for r in range(req_size)])

    around = jnp.stack([documents] + [along_y(documents, hop) for hop in range(1, tall)])
    around = jnp.stack([around] + [along_x(around, hop) for hop in range(1, width)])
    upward, downward = [around], [around]
    for _ in range(1, DEPTH):
        upward.append(lax.ppermute(upward[-1], "req", [(r, r + width) for r in range(req_size - width)]))
        downward.append(lax.ppermute(downward[-1], "req", [(r, r - width) for r in range(width, req_size)]))
    around = jnp.stack(
        [around] + [jnp.where(z >= hop, upward[hop], downward[DEPTH - hop]) for hop in range(1, DEPTH)]
    )
    pieces = jnp.stack([around, to_core(around)]).reshape(-1, shard_rows, P_SIZE)

    place = x % 2 + 2 * (z % 2)
    part_columns = up_weight.shape[1] // 4

    def part(weight, which):
        return lax.dynamic_slice_in_dim(weight, which * part_columns, part_columns, 1)

    own = [(up_weight, to_core(up_weight)), (down_weight, to_core(down_weight))]
    brought = [[], []]
    for hop in range(1, tall):
        for kind, weight in enumerate((up_weight, down_weight)):
            first = along_y(part(weight, place), hop)
            brought[kind] += [first, to_pair(first, 1), to_pair(first, width)]
        for kind, weight in enumerate((up_weight, down_weight)):
            brought[kind].append(along_y(part(weight, 3 - place), hop))
    far = [(jnp.concatenate(side, axis=1), jnp.concatenate([to_core(block) for block in side], axis=1)) for side in brought]

    normed = attend(tokens, attend_weight, output_weight, attend_gain, query_length)

    def feed(up, down):
        hidden = jax.nn.gelu(
            jnp.dot(normed, up, preferred_element_type=jnp.float32), approximate=False
        ).astype(jnp.bfloat16)
        return lax.dot_general(hidden, down, (((1,), (1,)), ((), ())), preferred_element_type=jnp.float32)

    reduced = feed(own[0][0], own[1][0]) + feed(own[0][1], own[1][1])
    reduced = reduced + feed(far[0][0], far[1][0]) + feed(far[0][1], far[1][1])
    layer_out = norm_rows(normed.astype(jnp.float32) + reduced, mlp_gain).astype(jnp.bfloat16)
    projected = jnp.dot(layer_out, embed_weight, preferred_element_type=jnp.float32)
    unit = projected * lax.rsqrt(jnp.sum(projected * projected, axis=-1, keepdims=True) + 1e-06)
    live_slot = jnp.arange(SEQ)[None, :] < query_length[:, None]
    embedded = jnp.where(live_slot.reshape(rows, 1), unit, 0.0).astype(jnp.bfloat16)

    lengths = lax.all_gather(document_length, "req", axis=0, tiled=True)
    limits = lengths[candidates]
    owner = candidates // held_docs
    parts = jnp.arange(mlp_size, dtype=jnp.int32)
    away_z = (z - owner // width) % DEPTH
    away_x = (x - owner % width) % width
    away_y = (y - parts // CORES) % tall
    away_core = (core + parts) % CORES
    spots = (away_core * DEPTH + away_z[..., None]) * width + away_x[..., None]
    spots = (spots * tall + away_y) * held_docs + (candidates % held_docs)[..., None]
    scores = score(embedded, pieces, spots.astype(jnp.int32), limits)
    return (embedded, scores)


def solution(mesh):
    return jax.shard_map(
        functools.partial(on_device, mesh.shape["req"], mesh.shape["mlp"]),
        mesh=mesh,
        in_specs=(
            P(("req", "mlp"), None),
            P(),
            P(),
            P(),
            P(None, "mlp"),
            P(None, "mlp"),
            P(),
            P(),
            P(("req", "mlp")),
            P("req", "mlp", None),
            P("req"),
            P(("req", "mlp"), None),
        ),
        out_specs=(P(("req", "mlp"), None), P(("req", "mlp"), None)),
        check_vma=False,
    )
```

time: 290 us -> 158 us (0.54)
  waiting for transfers between devices: 182 us -> 36.3 us
  starting transfers between devices: 5.67 us -> 32 us
  local copies, waits for them, and re-layouts: 29.5 us -> 10.7 us
  Pallas kernels: 0 us -> 14.2 us
  blocking collectives: 0 us -> 13.2 us
  between operations: 14 us -> 1.76 us
  matrix products: 53.2 us -> 42.2 us
    all_gather x3 -> x0, waiting for transfers between devices: 144 us -> none  [the longest x1 64 us: on_device(): lax.all_gather(embedded, ('req', 'mlp'), axis=0, tiled=True)]
    ppermute x0 -> x27, waiting for transfers between devices: none -> 36.3 us  [the longest x5 20.5 us: along_y(): lax.ppermute(block, 'mlp', [(m, (m + CORES * hops) % mlp_size) for m in r...]
    ppermute x0 -> x27, starting transfers between devices: none -> 32 us  [the longest x3 11.7 us: on_device(): lax.ppermute(upward[-1], 'req', [(r, r + width) for r in range(req_size -...]
    pmax x1 -> x0, waiting for transfers between devices: 30.5 us -> none  [on_device(): lax.pmax(partial_best.astype(jnp.bfloat16), 'mlp')]
    pallas_call x0 -> x2, Pallas kernels: none -> 14.2 us  [the longest x1 12.1 us: attend(): pl.pallas_call(attend_kernel, out_shape=jax.ShapeDtypeStruct((rows, D), j...]
    unnamed x0 -> x1, blocking collectives: none -> 13.2 us
    dot_general x6 -> x4, matrix products: 52.6 us -> 39.8 us  [feed(): lax.dot_general(hidden, down, (((1,), (1,)), ((), ())), preferred_element...]
    reshape x1 -> x0, local copies, waits for them, and re-layouts: 8.91 us -> none  [on_device(): packed = packed.reshape(requests, SEQ, 3, HEADS, HD)]
  transfers between devices with their start and end apart: 5 -> 27, of which waited for: 5 -> 4; matrix products, arithmetic and copies ran while one was open for 14% -> 32% of each run, Pallas kernels for 0% -> 8%
where the time goes in v1:
time: 158 us; the launch traced here: 157 us
  matrix products  42.2 us (27%)
  waiting for transfers between devices  36.3 us (23%)
  starting transfers between devices  32 us (20%)
  Pallas kernels  14.2 us (9%)
  blocking collectives  13.2 us (8%)
  local copies, waits for them, and re-layouts  10.7 us (7%)
  other arithmetic  7.17 us (5%)
  between operations  1.76 us (1%)
    dot_general x4, matrix products, feed(): lax.dot_general(hidden, down, (((1,), (1,)), ((), ())), preferred_element...  39.8 us
    ppermute x5, waiting for transfers between devices, along_y(): lax.ppermute(block, 'mlp', [(m, (m + CORES * hops) % mlp_size) for m in r...  20.5 us
    unnamed x1, blocking collectives  13.2 us
    pallas_call x1, Pallas kernels, attend(): pl.pallas_call(attend_kernel, out_shape=jax.ShapeDtypeStruct((rows, D), j...  12.1 us
    ppermute x4, waiting for transfers between devices, to_pair(): lax.ppermute(block, 'req', [(r, r ^ stride) for r in range(req_size)])  12 us
    ppermute x3, starting transfers between devices, on_device(): lax.ppermute(upward[-1], 'req', [(r, r + width) for r in range(req_size -...  11.7 us
    ppermute x5, starting transfers between devices, along_y(): lax.ppermute(block, 'mlp', [(m, (m + CORES * hops) % mlp_size) for m in r...  7.08 us
    unnamed x49, local copies, waits for them, and re-layouts  5.98 us
  transfers between devices with their start and end apart: 27, of which 4 were waited for; matrix products, arithmetic and copies ran while one was open for 32% of the time, Pallas kernels for 8%

profile of v1, /device:TPU:0, one launch (start us, length us, event | category | flops | bytes accessed | tf_op | source)
XLA Modules:
  0.0 157.5 jit_solution(439677416604199098)
XLA Ops:
  2.2 3.0 %collective-permute-start.9 = (bf16[1024,256]{1,0:T(8,128)(2,1)S(1)}, bf16[1024,256]{1,0:T(8,128)(2,1)}, u32[]{:S(2)}, u32[]{:S(2)}) collective-permute-start(bf16[1024,256]{1,0:T(8,128)(2,1)S(1)} %get-tuple-element.7), channel_id=1, source_target_pairs={{0,2},{1,3},{2,0},{3,1},{4,6},{5,7},{6,4},{7,5},{8,10},{9,11},{10,... | collective-permute-start | bytes 1572872 | tf_op jit(solution)/shard_map/ppermute | solution.py:153
  5.3 1.9 %collective-permute-start.18 = (bf16[8,64,128]{2,1,0:T(8,128)(2,1)S(1)}, bf16[8,64,128]{2,1,0:T(8,128)(2,1)S(1)}, u32[]{:S(2)}, u32[]{:S(2)}) collective-permute-start(bf16[8,64,128]{2,1,0:T(8,128)(2,1)S(1)} %copy-done.9), channel_id=1, source_target_pairs={{0,2},{1,3},{2,0},{3,1},{4,6},{5,7},{6,4},{7,5},{8,10},{9,11},{10,... | collective-permute-start | bytes 393224 | tf_op jit(solution)/shard_map/ppermute | solution.py:153
  7.3 2.3 %constant_dynamic-slice_fusion.3 = (bf16[1024,256]{1,0:T(8,128)(2,1)}, bf16[1024,256]{1,0:T(8,128)(2,1)}) fusion(bf16[1024,1024]{1,0:T(8,128)(2,1)} %param.16, s32[]{:T(128)S(6)} %select_n.118, s32[]{:T(128)S(6)} %select_n.119), kind=kLoop, calls=%fused_computation.294 | loop fusion | bytes 2097160 | tf_op jit(solution)/shard_map/dynamic_slice | solution.py:178
  9.6 1.9 %collective-permute-start.2 = (bf16[1024,256]{1,0:T(8,128)(2,1)}, bf16[1024,256]{1,0:T(8,128)(2,1)}, u32[]{:S(2)}, u32[]{:S(2)}) collective-permute-start(bf16[1024,256]{1,0:T(8,128)(2,1)} %get-tuple-element.4), channel_id=1, source_target_pairs={{0,2},{1,3},{2,0},{3,1},{4,6},{5,7},{6,4},{7,5},{8,10},{9,11},{10,... | collective-permute-start | bytes 1572872 | tf_op jit(solution)/shard_map/ppermute | solution.py:153
  11.6 20.5 %collective-permute-done.18 = bf16[8,64,128]{2,1,0:T(8,128)(2,1)S(1)} collective-permute-done((bf16[8,64,128]{2,1,0:T(8,128)(2,1)S(1)}, bf16[8,64,128]{2,1,0:T(8,128)(2,1)S(1)}, u32[]{:S(2)}, u32[]{:S(2)}) %collective-permute-start.18) | collective-permute-done | bytes 131104 | tf_op jit(solution)/shard_map/ppermute | solution.py:153
  32.1 2.1 %collective-permute-start.19 = (bf16[2,8,64,128]{3,2,1,0:T(8,128)(2,1)S(1)}, bf16[2,8,64,128]{3,2,1,0:T(8,128)(2,1)S(1)}, u32[]{:S(2)}, u32[]{:S(2)}) collective-permute-start(bf16[2,8,64,128]{3,2,1,0:T(8,128)(2,1)S(1)} %get-tuple-element.11), channel_id=1, source_target_pairs={{0,4},{4,0},{8,12},{12,8},{16,20},{20,16},{24,28},{28,24},{1,5},{5... | collective-permute-start | bytes 786440 | tf_op jit(solution)/shard_map/ppermute | solution.py:156
  34.2 2.8 %copy-done.2 = bf16[1024,3072]{1,0:T(8,128)(2,1)S(1)} copy-done((bf16[1024,3072]{1,0:T(8,128)(2,1)S(1)}, bf16[1024,3072]{1,0:T(8,128)(2,1)}, u32[]{:S(2)}) %copy-start.2) | copy-done | bytes 6291480
  37.0 12.1 %attend.1 = bf16[512,1024]{1,0:T(8,128)(2,1)S(1)} custom-call(s32[4]{0:T(128)S(1)} %copy-done.6, bf16[512,1024]{1,0:T(8,128)(2,1)S(1)} %copy-done.4, bf16[1024,3072]{1,0:T(8,128)(2,1)S(1)} %copy-done.2, bf16[1024,1024]{1,0:T(8,128)(2,1)S(1)} %copy-done.3, f32[1,1024]{1,0:T(1,128)S(1)} %bitcast.31), custom_call_target="tpu_custom_call" | custom-call | flops 4831838208 | bytes 10485760 | tf_op jit(solution)/shard_map/attend/pallas_call | solution.py:79
  49.2 3.7 %collective-permute-start.20 = (bf16[2,2,8,64,128]{4,3,2,1,0:T(8,128)(2,1)S(1)}, bf16[2,2,8,64,128]{4,3,2,1,0:T(8,128)(2,1)S(1)}, u32[]{:S(2)}, u32[]{:S(2)}) collective-permute-start(bf16[2,2,8,64,128]{4,3,2,1,0:T(8,128)(2,1)S(1)} %get-tuple-element.9), channel_id=1, source_target_pairs={{0,8},{4,12},{8,16},{12,20},{16,24},{20,28},{1,9},{5,13},{9,17},{1... | collective-permute-start | bytes 1572872 | tf_op jit(solution)/shard_map/ppermute | solution.py:167
  54.2 2.7 %collective-permute-start.8 = (bf16[1024,256]{1,0:T(8,128)(2,1)}, bf16[1024,256]{1,0:T(8,128)(2,1)}, u32[]{:S(2)}, u32[]{:S(2)}) collective-permute-start(bf16[1024,256]{1,0:T(8,128)(2,1)} %collective-permute-done.6), channel_id=1, source_target_pairs={{0,8},{4,12},{8,0},{12,4},{16,24},{20,28},{24,16},{28,20},{1,9},{5... | collective-permute-start | bytes 1572872 | tf_op jit(solution)/shard_map/ppermute | solution.py:161
  56.9 9.8 %fusion.82 = f32[512,1024]{1,0:T(8,128)} fusion(bf16[1024,1024]{1,0:T(8,128)(2,1)} %param.17, bf16[512,1024]{1,0:T(8,128)(2,1)S(1)} %attend.1, bf16[1024,1024]{1,0:T(8,128)(2,1)} %param.16), kind=kOutput, calls=%fused_computation.115 | convolution fusion | flops 2181562368 | bytes 7340032 | tf_op jit(solution)/shard_map/dot_general | solution.py:196
  68.3 13.2 %all-reduce = s32[64]{0:T(128)S(1)} all-reduce(s32[64]{0:T(128)S(1)} %dynamic-update-slice), channel_id=1, replica_groups=mesh['req'=8,'mlp'=4] {'req'}, use_global_device_ids=true, to_apply=%add | all-reduce | flops 64 | bytes 512
  84.5 4.7 %collective-permute-start.24 = (bf16[2,2,8,64,128]{4,3,2,1,0:T(8,128)(2,1)S(1)}, bf16[2,2,8,64,128]{4,3,2,1,0:T(8,128)(2,1)}, u32[]{:S(2)}, u32[]{:S(2)}) collective-permute-start(bf16[2,2,8,64,128]{4,3,2,1,0:T(8,128)(2,1)S(1)} %collective-permute-done.20), channel_id=1, source_target_pairs={{0,8},{4,12},{8,16},{12,20},{16,24},{20,28},{1,9},{5,13},{9,17},{1... | collective-permute-start | bytes 1572872 | tf_op jit(solution)/shard_map/ppermute | solution.py:167
  90.6 6.8 %collective-permute-done.7 = bf16[1024,256]{1,0:T(8,128)(2,1)S(1)} collective-permute-done((bf16[1024,256]{1,0:T(8,128)(2,1)}, bf16[1024,256]{1,0:T(8,128)(2,1)S(1)}, u32[]{:S(2)}, u32[]{:S(2)}) %collective-permute-start.7) | collective-permute-done | bytes 524320 | tf_op jit(solution)/shard_map/ppermute | solution.py:161
  98.0 5.1 %collective-permute-done.3 = bf16[1024,256]{1,0:T(8,128)(2,1)S(1)} collective-permute-done((bf16[1024,256]{1,0:T(8,128)(2,1)}, bf16[1024,256]{1,0:T(8,128)(2,1)S(1)}, u32[]{:S(2)}, u32[]{:S(2)}) %collective-permute-start.3) | collective-permute-done | bytes 524320 | tf_op jit(solution)/shard_map/ppermute | solution.py:161
  103.1 3.3 %collective-permute-start.25 = (bf16[2,2,8,64,128]{4,3,2,1,0:T(8,128)(2,1)}, bf16[2,2,8,64,128]{4,3,2,1,0:T(8,128)(2,1)}, u32[]{:S(2)}, u32[]{:S(2)}) collective-permute-start(bf16[2,2,8,64,128]{4,3,2,1,0:T(8,128)(2,1)} %collective-permute-done.24), channel_id=1, source_target_pairs={{0,8},{4,12},{8,16},{12,20},{16,24},{20,28},{1,9},{5,13},{9,17},{1... | collective-permute-start | bytes 1572872 | tf_op jit(solution)/shard_map/ppermute | solution.py:167
  107.9 9.7 %fusion.20 = f32[512,1024]{1,0:T(8,128)} fusion(bf16[1024,256]{1,0:T(8,128)(2,1)} %collective-permute-done.9, bf16[1024,256]{1,0:T(8,128)(2,1)} %collective-permute-done.8, bf16[1024,256]{1,0:T(8,128)(2,1)} %copy-done.12, bf16[1024,256]{1,0:T(8,128)(2,1)} %collective-permute-done.6, bf16[512,1024]{1,0:T(8,128)(2,1)S(1)} %attend.1, ...), kind=kOutput, calls=%fused_computation.26 | convolution fusion | flops 2198339584 | bytes 7340032 | tf_op jit(solution)/shard_map/dot_general | solution.py:196
  117.8 3.8 %collective-permute-done.23 = bf16[2,2,8,64,128]{4,3,2,1,0:T(8,128)(2,1)} collective-permute-done((bf16[2,2,8,64,128]{4,3,2,1,0:T(8,128)(2,1)S(1)}, bf16[2,2,8,64,128]{4,3,2,1,0:T(8,128)(2,1)}, u32[]{:S(2)}, u32[]{:S(2)}) %collective-permute-start.23) | collective-permute-done | bytes 524320 | tf_op jit(solution)/shard_map/ppermute | solution.py:168
  122.8 2.4 %fusion.349 = (bf16[1,4,2,2,8,64,128]{6,5,4,3,2,1,0:T(8,128)(2,1)}, bf16[4,2,2,8,64,128]{5,4,3,2,1,0:T(8,128)(2,1)}) fusion(bf16[1,2,2,8,64,128]{5,4,3,2,1,0:T(8,128)(2,1)S(1)} %select_bitcast_fusion, bf16[1,2,2,8,64,128]{5,4,3,2,1,0:T(8,128)(2,1)S(1)} %select_bitcast_fusion.1, bf16[1,2,2,8,64,128]{5,4,3,2,1,0:T(8,128)(2,1)S(1)} %select_bitcast_fusion.2, ...), kind=kLoop, calls=%fused_computation.424 | loop fusion | flops 3145728 | bytes 6291456 | tf_op jit(solution)/shard_map/stack | solution.py:172
  127.0 10.0 %fusion.80 = f32[512,1024]{1,0:T(8,128)} fusion(bf16[1024,1024]{1,0:T(8,128)(2,1)} %collective-permute-done.1, bf16[512,1024]{1,0:T(8,128)(2,1)S(1)} %attend.1, bf16[1024,1024]{1,0:T(8,128)(2,1)} %collective-permute-done), kind=kOutput, calls=%fused_computation.114 | convolution fusion | flops 2181562368 | bytes 7340032 | tf_op jit(solution)/shard_map/dot_general | solution.py:196
  137.8 10.4 %fusion.350 = (f32[512]{0:T(512)S(1)}, f32[512,1024]{1,0:T(8,128)S(1)}) fusion(bf16[1024,256]{1,0:T(8,128)(2,1)} %collective-permute-done.17, bf16[1024,256]{1,0:T(8,128)(2,1)} %collective-permute-done.16, bf16[1024,256]{1,0:T(8,128)(2,1)} %collective-permute-done.15, bf16[1024,256]{1,0:T(8,128)(2,1)} %copy-done.18, bf16[512,1024]{1,0:T(8,128)(2,1)S(1)} %attend.1, ...), kind=kOutput, calls=%fused_computation.425 | convolution fusion | flops 2201484800 | bytes 13633536 | tf_op jit(solution)/shard_map/dot_general | solution.py:196
  149.9 2.4 %multiply_reduce_fusion.1 = (f32[512]{0:T(512)S(1)}, f32[512,128]{0,1:T(8,128)S(1)}) fusion(bf16[1024,128]{1,0:T(8,128)(2,1)S(1)} %copy-done, f32[512,1024]{1,0:T(8,128)} %copy-done.8, f32[1024]{0:T(1024)S(1)} %copy-done.10, f32[512]{0:T(512)S(1)} %add_rsqrt_fusion.1, f32[512]{0:T(512)S(1)} %broadcast_multiply_fusion), kind=kOutput, calls=%fused_computation.246 | convolution fusion | flops 136445440 | bytes 2631680 | tf_op jit(solution)/shard_map/dot_general | solution.py:201
  152.7 2.0 %pad_maximum_fusion = bf16[2,4,2,2,8,64,128]{6,5,4,3,2,1,0:T(8,128)(2,1)S(1)} fusion(bf16[1,4,2,2,8,64,128]{6,5,4,3,2,1,0:T(8,128)(2,1)} %bitcast.12, bf16[1,4,2,2,8,64,128]{6,5,4,3,2,1,0:T(8,128)(2,1)S(1)} %copy-done.7), kind=kLoop, calls=%fused_computation.1 | loop fusion | flops 2097152 | bytes 8388608 | tf_op jit(solution)/shard_map/stack | solution.py:172
  154.7 2.1 %score.1 = f32[4,8,128]{2,1,0:T(8,128)S(1)} custom-call(s32[4,8,4]{2,1,0:T(8,128)S(1)} %multiply_add_fusion.spots_ref, s32[4,8]{1,0:T(4,128)S(1)} %reshape.92.limits_ref, bf16[512,128]{1,0:T(8,128)(2,1)S(1)} %select_convert_fusion.embedded_ref, bf16[256,64,128]{2,1,0:T(8,128)(2,1)S(1)} %bitcast.30), custom_call_target="tpu_custom_call" | custom-call | flops 268435456 | bytes 5242880 | tf_op jit(solution)/shard_map/score/pallas_call | solution.py:115
  (111 shorter events, 17.1 us)
Async XLA Ops:
  2.2 50.7 %collective-permute-start.9 = (bf16[1024,256]{1,0:T(8,128)(2,1)S(1)}, bf16[1024,256]{1,0:T(8,128)(2,1)}, u32[]{:S(2)}, u32[]{:S(2)}) collective-permute-start(bf16[1024,256]{1,0:T(8,128)(2,1)S(1)} %get-tuple-element.7), channel_id=1, source_target_pairs={{0,2},{1,3},{2,0},{3,1},{4,6},{5,7},{6,4},{7,5},{8,10},{9,11},{10,... | collective-permute-start | bytes 1572872 | tf_op jit(solution)/shard_map/ppermute | solution.py:153
  5.2 49.0 %collective-permute-start.6 = (bf16[1024,256]{1,0:T(8,128)(2,1)S(1)}, bf16[1024,256]{1,0:T(8,128)(2,1)}, u32[]{:S(2)}, u32[]{:S(2)}) collective-permute-start(bf16[1024,256]{1,0:T(8,128)(2,1)S(1)} %get-tuple-element.6), channel_id=1, source_target_pairs={{0,2},{1,3},{2,0},{3,1},{4,6},{5,7},{6,4},{7,5},{8,10},{9,11},{10,... | collective-permute-start | bytes 1572872 | tf_op jit(solution)/shard_map/ppermute | solution.py:153
  5.3 26.7 %collective-permute-start.18 = (bf16[8,64,128]{2,1,0:T(8,128)(2,1)S(1)}, bf16[8,64,128]{2,1,0:T(8,128)(2,1)S(1)}, u32[]{:S(2)}, u32[]{:S(2)}) collective-permute-start(bf16[8,64,128]{2,1,0:T(8,128)(2,1)S(1)} %copy-done.9), channel_id=1, source_target_pairs={{0,2},{1,3},{2,0},{3,1},{4,6},{5,7},{6,4},{7,5},{8,10},{9,11},{10,... | collective-permute-start | bytes 393224 | tf_op jit(solution)/shard_map/ppermute | solution.py:153
  9.5 72.8 %collective-permute-start.5 = (bf16[1024,256]{1,0:T(8,128)(2,1)}, bf16[1024,256]{1,0:T(8,128)(2,1)}, u32[]{:S(2)}, u32[]{:S(2)}) collective-permute-start(bf16[1024,256]{1,0:T(8,128)(2,1)} %get-tuple-element.5), channel_id=1, source_target_pairs={{0,2},{1,3},{2,0},{3,1},{4,6},{5,7},{6,4},{7,5},{8,10},{9,11},{10,... | collective-permute-start | bytes 1572872 | tf_op jit(solution)/shard_map/ppermute | solution.py:153
  9.6 73.2 %collective-permute-start.2 = (bf16[1024,256]{1,0:T(8,128)(2,1)}, bf16[1024,256]{1,0:T(8,128)(2,1)}, u32[]{:S(2)}, u32[]{:S(2)}) collective-permute-start(bf16[1024,256]{1,0:T(8,128)(2,1)} %get-tuple-element.4), channel_id=1, source_target_pairs={{0,2},{1,3},{2,0},{3,1},{4,6},{5,7},{6,4},{7,5},{8,10},{9,11},{10,... | collective-permute-start | bytes 1572872 | tf_op jit(solution)/shard_map/ppermute | solution.py:153
  32.1 17.0 %collective-permute-start.19 = (bf16[2,8,64,128]{3,2,1,0:T(8,128)(2,1)S(1)}, bf16[2,8,64,128]{3,2,1,0:T(8,128)(2,1)S(1)}, u32[]{:S(2)}, u32[]{:S(2)}) collective-permute-start(bf16[2,8,64,128]{3,2,1,0:T(8,128)(2,1)S(1)} %get-tuple-element.11), channel_id=1, source_target_pairs={{0,4},{4,0},{8,12},{12,8},{16,20},{20,16},{24,28},{28,24},{1,5},{5... | collective-permute-start | bytes 786440 | tf_op jit(solution)/shard_map/ppermute | solution.py:156
  49.2 33.6 %collective-permute-start.20 = (bf16[2,2,8,64,128]{4,3,2,1,0:T(8,128)(2,1)S(1)}, bf16[2,2,8,64,128]{4,3,2,1,0:T(8,128)(2,1)S(1)}, u32[]{:S(2)}, u32[]{:S(2)}) collective-permute-start(bf16[2,2,8,64,128]{4,3,2,1,0:T(8,128)(2,1)S(1)} %get-tuple-element.9), channel_id=1, source_target_pairs={{0,8},{4,12},{8,16},{12,20},{16,24},{20,28},{1,9},{5,13},{9,17},{1... | collective-permute-start | bytes 1572872 | tf_op jit(solution)/shard_map/ppermute | solution.py:167
  52.9 31.6 %collective-permute-start.21 = (bf16[2,2,8,64,128]{4,3,2,1,0:T(8,128)(2,1)S(1)}, bf16[2,2,8,64,128]{4,3,2,1,0:T(8,128)(2,1)S(1)}, u32[]{:S(2)}, u32[]{:S(2)}) collective-permute-start(bf16[2,2,8,64,128]{4,3,2,1,0:T(8,128)(2,1)S(1)} %get-tuple-element.9), channel_id=1, source_target_pairs={{8,0},{12,4},{16,8},{20,12},{24,16},{28,20},{9,1},{13,5},{17,9},{2... | collective-permute-start | bytes 1572872 | tf_op jit(solution)/shard_map/ppermute | solution.py:168
  54.2 34.9 %collective-permute-start.8 = (bf16[1024,256]{1,0:T(8,128)(2,1)}, bf16[1024,256]{1,0:T(8,128)(2,1)}, u32[]{:S(2)}, u32[]{:S(2)}) collective-permute-start(bf16[1024,256]{1,0:T(8,128)(2,1)} %collective-permute-done.6), channel_id=1, source_target_pairs={{0,8},{4,12},{8,0},{12,4},{16,24},{20,28},{24,16},{28,20},{1,9},{5... | collective-permute-start | bytes 1572872 | tf_op jit(solution)/shard_map/ppermute | solution.py:161
  82.3 15.1 %collective-permute-start.7 = (bf16[1024,256]{1,0:T(8,128)(2,1)}, bf16[1024,256]{1,0:T(8,128)(2,1)S(1)}, u32[]{:S(2)}, u32[]{:S(2)}) collective-permute-start(bf16[1024,256]{1,0:T(8,128)(2,1)} %collective-permute-done.6), channel_id=1, source_target_pairs={{0,4},{4,0},{8,12},{12,8},{16,20},{20,16},{24,28},{28,24},{1,5},{5... | collective-permute-start | bytes 1572872 | tf_op jit(solution)/shard_map/ppermute | solution.py:161
  82.8 14.6 %collective-permute-start.4 = (bf16[1024,256]{1,0:T(8,128)(2,1)}, bf16[1024,256]{1,0:T(8,128)(2,1)S(1)}, u32[]{:S(2)}, u32[]{:S(2)}) collective-permute-start(bf16[1024,256]{1,0:T(8,128)(2,1)} %collective-permute-done.2), channel_id=1, source_target_pairs={{0,8},{4,12},{8,0},{12,4},{16,24},{20,28},{24,16},{28,20},{1,9},{5... | collective-permute-start | bytes 1572872 | tf_op jit(solution)/shard_map/ppermute | solution.py:161
  82.8 20.3 %collective-permute-start.3 = (bf16[1024,256]{1,0:T(8,128)(2,1)}, bf16[1024,256]{1,0:T(8,128)(2,1)S(1)}, u32[]{:S(2)}, u32[]{:S(2)}) collective-permute-start(bf16[1024,256]{1,0:T(8,128)(2,1)} %collective-permute-done.2), channel_id=1, source_target_pairs={{0,4},{4,0},{8,12},{12,8},{16,20},{20,16},{24,28},{28,24},{1,5},{5... | collective-permute-start | bytes 1572872 | tf_op jit(solution)/shard_map/ppermute | solution.py:161
  84.5 18.6 %collective-permute-start.24 = (bf16[2,2,8,64,128]{4,3,2,1,0:T(8,128)(2,1)S(1)}, bf16[2,2,8,64,128]{4,3,2,1,0:T(8,128)(2,1)}, u32[]{:S(2)}, u32[]{:S(2)}) collective-permute-start(bf16[2,2,8,64,128]{4,3,2,1,0:T(8,128)(2,1)S(1)} %collective-permute-done.20), channel_id=1, source_target_pairs={{0,8},{4,12},{8,16},{12,20},{16,24},{20,28},{1,9},{5,13},{9,17},{1... | collective-permute-start | bytes 1572872 | tf_op jit(solution)/shard_map/ppermute | solution.py:167
  89.1 17.3 %collective-permute-start.22 = (bf16[2,2,8,64,128]{4,3,2,1,0:T(8,128)(2,1)S(1)}, bf16[2,2,8,64,128]{4,3,2,1,0:T(8,128)(2,1)S(1)}, u32[]{:S(2)}, u32[]{:S(2)}) collective-permute-start(bf16[2,2,8,64,128]{4,3,2,1,0:T(8,128)(2,1)S(1)} %collective-permute-done.21), channel_id=1, source_target_pairs={{8,0},{12,4},{16,8},{20,12},{24,16},{28,20},{9,1},{13,5},{17,9},{2... | collective-permute-start | bytes 1572872 | tf_op jit(solution)/shard_map/ppermute | solution.py:168
  97.4 28.8 %collective-permute-start.1 = (bf16[1024,1024]{1,0:T(8,128)(2,1)}, bf16[1024,1024]{1,0:T(8,128)(2,1)}, u32[]{:S(2)}, u32[]{:S(2)}) collective-permute-start(bf16[1024,1024]{1,0:T(8,128)(2,1)} %param.17), channel_id=1, source_target_pairs={{0,1},{1,0},{2,3},{3,2},{4,5},{5,4},{6,7},{7,6},{8,9},{9,8},{10,11... | collective-permute-start | bytes 6291464 | tf_op jit(solution)/shard_map/ppermute | solution.py:150
  97.5 29.0 %collective-permute-start = (bf16[1024,1024]{1,0:T(8,128)(2,1)}, bf16[1024,1024]{1,0:T(8,128)(2,1)}, u32[]{:S(2)}, u32[]{:S(2)}) collective-permute-start(bf16[1024,1024]{1,0:T(8,128)(2,1)} %param.16), channel_id=1, source_target_pairs={{0,1},{1,0},{2,3},{3,2},{4,5},{5,4},{6,7},{7,6},{8,9},{9,8},{10,11... | collective-permute-start | bytes 6291464 | tf_op jit(solution)/shard_map/ppermute | solution.py:150
  103.1 22.0 %collective-permute-start.17 = (bf16[1024,256]{1,0:T(8,128)(2,1)}, bf16[1024,256]{1,0:T(8,128)(2,1)}, u32[]{:S(2)}, u32[]{:S(2)}) collective-permute-start(bf16[1024,256]{1,0:T(8,128)(2,1)} %collective-permute-done.9), channel_id=1, source_target_pairs={{0,1},{1,0},{2,3},{3,2},{4,5},{5,4},{6,7},{7,6},{8,9},{9,8},{10,11... | collective-permute-start | bytes 1572872 | tf_op jit(solution)/shard_map/ppermute | solution.py:150
  103.1 14.6 %collective-permute-start.25 = (bf16[2,2,8,64,128]{4,3,2,1,0:T(8,128)(2,1)}, bf16[2,2,8,64,128]{4,3,2,1,0:T(8,128)(2,1)}, u32[]{:S(2)}, u32[]{:S(2)}) collective-permute-start(bf16[2,2,8,64,128]{4,3,2,1,0:T(8,128)(2,1)} %collective-permute-done.24), channel_id=1, source_target_pairs={{0,8},{4,12},{8,16},{12,20},{16,24},{20,28},{1,9},{5,13},{9,17},{1... | collective-permute-start | bytes 1572872 | tf_op jit(solution)/shard_map/ppermute | solution.py:167
  106.5 15.1 %collective-permute-start.23 = (bf16[2,2,8,64,128]{4,3,2,1,0:T(8,128)(2,1)S(1)}, bf16[2,2,8,64,128]{4,3,2,1,0:T(8,128)(2,1)}, u32[]{:S(2)}, u32[]{:S(2)}) collective-permute-start(bf16[2,2,8,64,128]{4,3,2,1,0:T(8,128)(2,1)S(1)} %collective-permute-done.22), channel_id=1, source_target_pairs={{8,0},{12,4},{16,8},{20,12},{24,16},{28,20},{9,1},{13,5},{17,9},{2... | collective-permute-start | bytes 1572872 | tf_op jit(solution)/shard_map/ppermute | solution.py:168
  125.1 11.8 %collective-permute-start.10 = (bf16[1024,256]{1,0:T(8,128)(2,1)}, bf16[1024,256]{1,0:T(8,128)(2,1)S(1)}, u32[]{:S(2)}, u32[]{:S(2)}) collective-permute-start(bf16[1024,256]{1,0:T(8,128)(2,1)} %collective-permute-done.2), channel_id=1, source_target_pairs={{0,1},{1,0},{2,3},{3,2},{4,5},{5,4},{6,7},{7,6},{8,9},{9,8},{10,11... | collective-permute-start | bytes 1572872 | tf_op jit(solution)/shard_map/ppermute | solution.py:150
  125.7 11.5 %collective-permute-start.16 = (bf16[1024,256]{1,0:T(8,128)(2,1)}, bf16[1024,256]{1,0:T(8,128)(2,1)}, u32[]{:S(2)}, u32[]{:S(2)}) collective-permute-start(bf16[1024,256]{1,0:T(8,128)(2,1)} %collective-permute-done.8), channel_id=1, source_target_pairs={{0,1},{1,0},{2,3},{3,2},{4,5},{5,4},{6,7},{7,6},{8,9},{9,8},{10,11... | collective-permute-start | bytes 1572872 | tf_op jit(solution)/shard_map/ppermute | solution.py:150
  125.7 11.4 %collective-permute-start.15 = (bf16[1024,256]{1,0:T(8,128)(2,1)S(1)}, bf16[1024,256]{1,0:T(8,128)(2,1)}, u32[]{:S(2)}, u32[]{:S(2)}) collective-permute-start(bf16[1024,256]{1,0:T(8,128)(2,1)S(1)} %copy-done.13), channel_id=1, source_target_pairs={{0,1},{1,0},{2,3},{3,2},{4,5},{5,4},{6,7},{7,6},{8,9},{9,8},{10,11... | collective-permute-start | bytes 1572872 | tf_op jit(solution)/shard_map/ppermute | solution.py:150
  126.7 11.1 %collective-permute-start.11 = (bf16[1024,256]{1,0:T(8,128)(2,1)S(1)}, bf16[1024,256]{1,0:T(8,128)(2,1)}, u32[]{:S(2)}, u32[]{:S(2)}) collective-permute-start(bf16[1024,256]{1,0:T(8,128)(2,1)S(1)} %copy-done.17), channel_id=1, source_target_pairs={{0,1},{1,0},{2,3},{3,2},{4,5},{5,4},{6,7},{7,6},{8,9},{9,8},{10,11... | collective-permute-start | bytes 1572872 | tf_op jit(solution)/shard_map/ppermute | solution.py:150
  136.9 15.7 %collective-permute-start.26 = (bf16[4,2,2,8,64,128]{5,4,3,2,1,0:T(8,128)(2,1)}, bf16[4,2,2,8,64,128]{5,4,3,2,1,0:T(8,128)(2,1)}, u32[]{:S(2)}, u32[]{:S(2)}) collective-permute-start(bf16[4,2,2,8,64,128]{5,4,3,2,1,0:T(8,128)(2,1)} %get-tuple-element.3), channel_id=1, source_target_pairs={{0,1},{1,0},{2,3},{3,2},{4,5},{5,4},{6,7},{7,6},{8,9},{9,8},{10,11... | collective-permute-start | bytes 6291464 | tf_op jit(solution)/shard_map/ppermute | solution.py:150
  (26 other events, 409.8 us)

commit v2 on v1

v2 whole, which is shorter than its diff:
```python
import functools

import jax
import jax.numpy as jnp
from jax import lax
from jax.experimental import pallas as pl
from jax.experimental.pallas import tpu as pltpu
from jax.sharding import PartitionSpec as P

D = 1024
HEADS = 16
HD = 64
P_SIZE = 128
SEQ = 128
CORES = 2
DEPTH = 4
MIB = 1024 * 1024


def norm_rows(values, scaling):
    average = jnp.mean(values, axis=-1, keepdims=True)
    centred = values - average
    variance = jnp.mean(centred * centred, axis=-1, keepdims=True)
    return centred * lax.rsqrt(variance + 1e-05) * scaling


def pack_kernel(tokens_ref, attend_ref, *refs):
    packed = refs[-1]
    wide = 512

    def project(step, carry):
        columns = pl.ds(pl.multiple_of(step * wide, wide), wide)
        packed[:, columns] = jnp.dot(
            tokens_ref[...], attend_ref[:, columns], preferred_element_type=jnp.float32
        ).astype(jnp.bfloat16)
        return carry

    lax.fori_loop(0, 3 * D // wide, project, 0)


def attend_kernel(length_ref, packed, tokens_ref, output_ref, gain_ref, *refs):
    normed_ref, context = refs[-2:]
    rows = tokens_ref.shape[0]
    lane = lax.broadcasted_iota(jnp.int32, (SEQ, 2 * HD), 1)
    low = lane < HD
    key_slot = lax.broadcasted_iota(jnp.int32, (2 * SEQ, SEQ), 1)

    def one_request(request, carry):
        here = pl.ds(pl.multiple_of(request * SEQ, SEQ), SEQ)
        live = key_slot < length_ref[request]
        for pair in range(HEADS // 2):
            at = pair * 2 * HD
            query = packed[here, at : at + 2 * HD]
            keys = packed[here, D + at : D + at + 2 * HD]
            value = packed[here, 2 * D + at : 2 * D + at + 2 * HD]
            none = jnp.zeros_like(query)
            both = jnp.concatenate([jnp.where(low, query, none), jnp.where(low, none, query)], axis=0)
            logits = lax.dot_general(
                both, keys, (((1,), (1,)), ((), ())), preferred_element_type=jnp.float32
            ) * HD ** (-0.5)
            logits = jnp.where(live, logits, -1e30)
            weights = jnp.exp(logits - jnp.max(logits, axis=-1, keepdims=True))
            probs = (weights / jnp.sum(weights, axis=-1, keepdims=True)).astype(jnp.bfloat16)
            mixed = jnp.dot(probs, value, preferred_element_type=jnp.float32)
            context[here, at : at + 2 * HD] = jnp.where(low, mixed[:SEQ], mixed[SEQ:]).astype(jnp.bfloat16)
        return carry

    lax.fori_loop(0, rows // SEQ, one_request, 0)

    def finish(step, carry):
        here = pl.ds(pl.multiple_of(step * SEQ, SEQ), SEQ)
        attended = jnp.dot(context[here, :], output_ref[...], preferred_element_type=jnp.float32)
        normed_ref[here, :] = norm_rows(
            tokens_ref[here, :].astype(jnp.float32) + attended, gain_ref[...]
        ).astype(jnp.bfloat16)
        return carry

    lax.fori_loop(0, rows // SEQ, finish, 0)


def gate(values, awaited):
    anywhere = pl.BlockSpec(memory_space=pl.ANY)
    return pl.pallas_call(
        lambda *refs: None,
        out_shape=[jax.ShapeDtypeStruct(value.shape, value.dtype) for value in values],
        in_specs=[anywhere] * (len(values) + len(awaited)),
        out_specs=[anywhere] * len(values),
        input_output_aliases={at: at for at in range(len(values))},
        compiler_params=pltpu.CompilerParams(vmem_limit_bytes=MIB),
        name="gate",
    )(*values, *awaited)


def pack(tokens, attend_weight, awaited):
    rows = tokens.shape[0]
    vmem, anywhere = pl.BlockSpec(memory_space=pltpu.VMEM), pl.BlockSpec(memory_space=pl.ANY)
    return pl.pallas_call(
        pack_kernel,
        out_shape=jax.ShapeDtypeStruct((rows, 3 * D), jnp.bfloat16),
        in_specs=[vmem] * 2 + [anywhere] * len(awaited),
        out_specs=vmem,
        compiler_params=pltpu.CompilerParams(vmem_limit_bytes=32 * MIB),
        cost_estimate=pl.CostEstimate(flops=rows * D * D * 6, bytes_accessed=10 * MIB, transcendentals=0),
        name="pack",
    )(tokens, attend_weight, *awaited)


def attend(packed, tokens, output_weight, attend_gain, query_length, awaited):
    rows = tokens.shape[0]
    vmem, anywhere = pl.BlockSpec(memory_space=pltpu.VMEM), pl.BlockSpec(memory_space=pl.ANY)
    return pl.pallas_call(
        attend_kernel,
        out_shape=jax.ShapeDtypeStruct((rows, D), jnp.bfloat16),
        in_specs=[pl.BlockSpec(memory_space=pltpu.SMEM)] + [vmem] * 4 + [anywhere] * len(awaited),
        out_specs=vmem,
        scratch_shapes=[pltpu.VMEM((rows, D), jnp.bfloat16)],
        compiler_params=pltpu.CompilerParams(vmem_limit_bytes=32 * MIB),
        cost_estimate=pl.CostEstimate(flops=rows * D * D * 6, bytes_accessed=8 * MIB, transcendentals=rows * SEQ * HEADS),
        name="attend",
    )(query_length, packed, tokens, output_weight, attend_gain.reshape(1, D), *awaited)


def feed_kernel(dims, last, awaited, carried, *refs):
    refs = list(refs)
    out_ref = refs.pop()
    refs = refs[: len(refs) - awaited]
    normed_ref = refs.pop(0)
    if last:
        length_ref, gain_ref, embed_ref = refs.pop(0), refs.pop(0), refs.pop(0)
    before = refs.pop(0) if carried else None
    step = 256
    total = None if before is None else before[...]
    pairs = []
    if dims == 2:
        for at in range(0, refs[0].shape[1], step):
            pairs.append((refs[0].at[:, at : at + step], refs[1].at[:, at : at + step]))
    else:
        for ref in refs:
            pairs.append((ref.at[0], ref.at[1]))
    for up, down in pairs:
        inner = jnp.dot(normed_ref[...], up[...], preferred_element_type=jnp.float32)
        hidden = (0.5 * inner * (1.0 + lax.erf(inner * 0.5**0.5))).astype(jnp.bfloat16)
        term = lax.dot_general(hidden, down[...], (((1,), (1,)), ((), ())), preferred_element_type=jnp.float32)
        total = term if total is None else total + term
    if not last:
        out_ref[...] = total
        return
    layer_out = norm_rows(normed_ref[...].astype(jnp.float32) + total, gain_ref[...]).astype(jnp.bfloat16)
    projected = jnp.dot(layer_out, embed_ref[...], preferred_element_type=jnp.float32)
    unit = projected * lax.rsqrt(jnp.sum(projected * projected, axis=-1, keepdims=True) + 1e-06)
    slot = lax.broadcasted_iota(jnp.int32, (SEQ, P_SIZE), 0)
    for request in range(unit.shape[0] // SEQ):
        block = unit[request * SEQ : (request + 1) * SEQ]
        out_ref[request * SEQ : (request + 1) * SEQ, :] = jnp.where(
            slot < length_ref[request], block, 0.0
        ).astype(jnp.bfloat16)


def feed(normed, weights, before=None, ending=None, awaited=()):
    rows = normed.shape[0]
    smem, vmem = pl.BlockSpec(memory_space=pltpu.SMEM), pl.BlockSpec(memory_space=pltpu.VMEM)
    args, specs = [normed], [vmem]
    if ending is not None:
        args += list(ending)
        specs += [smem, vmem, vmem]
    if before is not None:
        args.append(before)
        specs.append(vmem)
    args += weights
    specs += [vmem] * len(weights) + [pl.BlockSpec(memory_space=pl.ANY)] * len(awaited)
    if ending is None:
        shape = jax.ShapeDtypeStruct((rows, D), jnp.float32)
    else:
        shape = jax.ShapeDtypeStruct((rows, P_SIZE), jnp.bfloat16)
    units = sum(weight.size for weight in weights) // (2 * D)
    return pl.pallas_call(
        functools.partial(feed_kernel, weights[0].ndim, ending is not None, len(awaited), before is not None),
        out_shape=shape,
        in_specs=specs,
        out_specs=vmem,
        compiler_params=pltpu.CompilerParams(vmem_limit_bytes=40 * MIB),
        cost_estimate=pl.CostEstimate(flops=4 * rows * D * units, bytes_accessed=8 * MIB, transcendentals=rows * units),
        name="feed",
    )(*args, *awaited)


def score_kernel(spots_ref, marks_ref, rows_ref, embedded_ref, pieces_ref, best_ref):
    requests, picks, parts = spots_ref.shape
    piece_rows = pieces_ref.shape[1]
    position = lax.broadcasted_iota(jnp.int32, (parts * piece_rows, SEQ), 0).astype(jnp.float32)
    row = lax.broadcasted_iota(jnp.int32, (piece_rows, P_SIZE), 0)

    def one_request(request, carry):
        block = embedded_ref[pl.ds(pl.multiple_of(request * SEQ, SEQ), SEQ), :]
        found = []
        for pick in range(picks):
            chosen = jnp.concatenate([pieces_ref[spots_ref[request, pick, part]] for part in range(parts)], axis=0)
            listed = pieces_ref[marks_ref[request, pick]].astype(jnp.float32)
            limit = jnp.sum(jnp.where(row == rows_ref[request, pick], listed, 0.0), axis=0, keepdims=True)
            sims = lax.dot_general(
                chosen, block, (((1,), (1,)), ((), ())), preferred_element_type=jnp.float32
            )
            sims = jnp.where(position < limit, sims, -1e30)
            found.append(jnp.max(sims, axis=0, keepdims=True))
        best_ref[request] = jnp.concatenate(found, axis=0)
        return carry

    lax.fori_loop(0, requests, one_request, 0)


def score(embedded, pieces, spots, marks, rows):
    requests, picks, parts = spots.shape
    smem, vmem = pl.BlockSpec(memory_space=pltpu.SMEM), pl.BlockSpec(memory_space=pltpu.VMEM)
    best = pl.pallas_call(
        score_kernel,
        out_shape=jax.ShapeDtypeStruct((requests, picks, SEQ), jnp.float32),
        in_specs=[smem, smem, smem, vmem, vmem],
        out_specs=vmem,
        compiler_params=pltpu.CompilerParams(vmem_limit_bytes=32 * MIB),
        cost_estimate=pl.CostEstimate(flops=2 * requests * picks * 256 * SEQ * P_SIZE, bytes_accessed=5 * MIB, transcendentals=0),
        name="score",
    )(spots, marks, rows, embedded, pieces)
    return jnp.sum(best, axis=2)


def on_device(
    req_size,
    mlp_size,
    tokens,
    attend_weight,
    output_weight,
    attend_gain,
    up_weight,
    down_weight,
    mlp_gain,
    embed_weight,
    query_length,
    documents,
    document_length,
    candidates,
):
    rows = tokens.shape[0]
    held_docs, shard_rows = documents.shape[:2]
    width, tall = req_size // DEPTH, mlp_size // CORES
    req, mlp = lax.axis_index("req"), lax.axis_index("mlp")
    z, x, y, core = req // width, req % width, mlp // CORES, mlp % CORES

    def to_core(block):
        return lax.ppermute(block, "mlp", [(m, m ^ 1) for m in range(mlp_size)])

    def along_y(block, hops):
        return lax.ppermute(block, "mlp", [(m, (m + CORES * hops) % mlp_size) for m in range(mlp_size)])

    def along_x(block, hops):
        return lax.ppermute(
            block, "req", [(r, r // width * width + (r % width + hops) % width) for r in range(req_size)]
        )

    def to_pair(block, stride):
        return lax.ppermute(block, "req", [(r, r ^ stride) for r in range(req_size)])

    listed = jnp.zeros((shard_rows, P_SIZE), jnp.bfloat16)
    listed = listed.at[:held_docs].set(document_length.astype(jnp.bfloat16)[:, None])
    block = jnp.concatenate([documents, listed[None]], axis=0)
    held = held_docs + 1
    upward, downward = [block], [block]
    for _ in range(1, DEPTH):
        upward.append(lax.ppermute(upward[-1], "req", [(r, r + width) for r in range(req_size - width)]))
        downward.append(lax.ppermute(downward[-1], "req", [(r, r - width) for r in range(width, req_size)]))
    around = jnp.stack(
        [block] + [jnp.where(z >= hop, upward[hop], downward[DEPTH - hop]) for hop in range(1, DEPTH)]
    )
    from_x = [along_x(around, hop) for hop in range(1, width)]

    place = x % 2 + 2 * (z % 2)
    part_columns = up_weight.shape[1] // 4

    def part(which):
        return jnp.stack(
            [lax.dynamic_slice_in_dim(w, which * part_columns, part_columns, 1) for w in (up_weight, down_weight)]
        )

    near = part(place)
    firsts = [along_y(near, hop) for hop in range(1, tall)]
    partner = [to_core(up_weight), to_core(down_weight)]


    packed = pack(tokens, attend_weight, [])
    normed = attend(packed, tokens, output_weight, attend_gain, query_length, [])
    around = jnp.stack([around] + from_x)
    held_back = gate([around] + firsts, [normed])
    around, firsts = held_back[0], held_back[1:]
    total = feed(normed, [up_weight, down_weight])
    total = feed(normed, partner, total)
    quarters = []
    for first in firsts:
        quarters += [first, to_pair(first, 1), to_pair(first, width)]
    around = jnp.stack([around] + [along_y(around, hop) for hop in range(1, tall)])
    quarters = gate(quarters, [total])
    halves = []
    for at in range(0, len(quarters), 3):
        halves.append(to_pair(quarters[at + 1][:, :, : part_columns // 2], width))
        halves.append(to_pair(quarters[at + 2][:, :, part_columns // 2 :], 1))
    passed = [to_core(quarter) for quarter in quarters]
    for at in range(0, len(quarters), 3):
        total = feed(normed, quarters[at : at + 3], total)
        total = feed(normed, passed[at : at + 3], total)
    held_back = gate([around] + halves, [total])
    around, halves = held_back[0], held_back[1:]
    pieces = jnp.stack([around, to_core(around)]).reshape(-1, shard_rows, P_SIZE)
    passed = [to_core(half) for half in halves]
    total = feed(normed, halves, total)
    ending = (query_length, mlp_gain.reshape(1, D), embed_weight)
    embedded = feed(normed, passed, total, ending)

    owner = candidates // held_docs
    parts = jnp.arange(mlp_size, dtype=jnp.int32)
    away_z = (z - owner // width) % DEPTH
    away_x = (x - owner % width) % width
    away_y = (y - parts // CORES) % tall
    away_core = (core + parts) % CORES
    spots = (away_core * tall + away_y) * width + away_x[..., None]
    spots = ((spots * DEPTH + away_z[..., None]) * held).astype(jnp.int32)
    places = (candidates % held_docs).astype(jnp.int32)
    scores = score(embedded, pieces, spots + places[..., None], spots[..., 0] + held_docs, places)
    return (embedded, scores)


def solution(mesh):
    return jax.shard_map(
        functools.partial(on_device, mesh.shape["req"], mesh.shape["mlp"]),
        mesh=mesh,
        in_specs=(
            P(("req", "mlp"), None),
            P(),
            P(),
            P(),
            P(None, "mlp"),
            P(None, "mlp"),
            P(),
            P(),
            P(("req", "mlp")),
            P("req", "mlp", None),
            P("req"),
            P(("req", "mlp"), None),
        ),
        out_specs=(P(("req", "mlp"), None), P(("req", "mlp"), None)),
        check_vma=False,
    )
```

time: 158 us -> 106 us (0.67)
  matrix products: 42.2 us -> 0 us
  Pallas kernels: 14.2 us -> 35.4 us
  blocking collectives: 13.2 us -> 0 us
  waiting for transfers between devices: 36.3 us -> 24.8 us
  local copies, waits for them, and re-layouts: 10.7 us -> 6.75 us
  starting transfers between devices: 32 us -> 29.2 us
    dot_general x5 -> x0, matrix products: 42.2 us -> none  [the longest x4 39.8 us: feed(): lax.dot_general(hidden, down, (((1,), (1,)), ((), ())), preferred_element...]
    pallas_call x0 -> x10, Pallas kernels: none -> 25.3 us  [the longest x6 21 us: feed(): pl.pallas_call(functools.partial(feed_kernel, weights[0].ndim, ending is...]
    ppermute x5 -> x2, waiting for transfers between devices: 20.5 us -> 1.66 us  [along_y(): lax.ppermute(block, 'mlp', [(m, (m + CORES * hops) % mlp_size) for m in r...]
    unnamed x1 -> x0, blocking collectives: 13.2 us -> none
    ppermute x4, waiting for transfers between devices: 12 us -> 18.4 us  [to_pair(): lax.ppermute(block, 'req', [(r, r ^ stride) for r in range(req_size)])]
    ppermute x5 -> x2, starting transfers between devices: 7.08 us -> 2.02 us  [along_y(): lax.ppermute(block, 'mlp', [(m, (m + CORES * hops) % mlp_size) for m in r...]
    pallas_call x1, Pallas kernels: 12.1 us -> 8 us  [attend(): pl.pallas_call(attend_kernel, out_shape=jax.ShapeDtypeStruct((rows, D), j...]
    dynamic_slice x2 -> x0, local copies, waits for them, and re-layouts: 3.7 us -> none  [part(): lax.dynamic_slice_in_dim(weight, which * part_columns, part_columns, 1)]
  transfers between devices with their start and end apart: 27 -> 21, of which waited for: 4 -> 9; matrix products, arithmetic and copies ran while one was open for 32% -> 6% of each run, Pallas kernels for 8% -> 32%
where the time goes in v2:
time: 106 us; the launch traced here: 105 us
  Pallas kernels  35.4 us (33%)
  starting transfers between devices  29.2 us (28%)
  waiting for transfers between devices  24.8 us (23%)
  other arithmetic  8.03 us (8%)
  local copies, waits for them, and re-layouts  6.75 us (6%)
    pallas_call x6, Pallas kernels, feed(): pl.pallas_call(functools.partial(feed_kernel, weights[0].ndim, ending is...  21 us
    ppermute x4, waiting for transfers between devices, to_pair(): lax.ppermute(block, 'req', [(r, r ^ stride) for r in range(req_size)])  18.4 us
    ppermute x3, starting transfers between devices, on_device(): lax.ppermute(upward[-1], 'req', [(r, r + width) for r in range(req_size -...  14.6 us
    pallas_call x1, Pallas kernels, attend(): pl.pallas_call(attend_kernel, out_shape=jax.ShapeDtypeStruct((rows, D), j...  8 us
    ppermute x4, starting transfers between devices, to_pair(): lax.ppermute(block, 'req', [(r, r ^ stride) for r in range(req_size)])  5.59 us
    unnamed x28, local copies, waits for them, and re-layouts  4.44 us
    pallas_call x1, Pallas kernels, pack(): pl.pallas_call(pack_kernel, out_shape=jax.ShapeDtypeStruct((rows, 3 * D),...  4.28 us
    ppermute x3, starting transfers between devices, on_device(): lax.ppermute(downward[-1], 'req', [(r, r - width) for r in range(width, r...  3.87 us
  transfers between devices with their start and end apart: 21, of which 9 were waited for; matrix products, arithmetic and copies ran while one was open for 6% of the time, Pallas kernels for 32%

profile of v2, /device:TPU:0, one launch (start us, length us, event | category | flops | bytes accessed | tf_op | source)
XLA Modules:
  0.0 105.3 jit_solution(17885960592093092999)
XLA Ops:
  2.3 4.9 %collective-permute-start.2 = (bf16[9,64,128]{2,1,0:T(8,128)(2,1)S(1)}, bf16[9,64,128]{2,1,0:T(8,128)(2,1)S(1)}, u32[]{:S(2)}, u32[]{:S(2)}) collective-permute-start(bf16[9,64,128]{2,1,0:T(8,128)(2,1)S(1)} %get-tuple-element.33), channel_id=1, source_target_pairs={{0,8},{4,12},{8,16},{12,20},{16,24},{20,28},{1,9},{5,13},{9,17},{1... | collective-permute-start | bytes 442376 | tf_op jit(solution)/shard_map/ppermute | solution.py:268
  10.3 5.1 %collective-permute-start.6 = (bf16[9,64,128]{2,1,0:T(8,128)(2,1)S(1)}, bf16[9,64,128]{2,1,0:T(8,128)(2,1)}, u32[]{:S(2)}, u32[]{:S(2)}) collective-permute-start(bf16[9,64,128]{2,1,0:T(8,128)(2,1)S(1)} %collective-permute-done.2), channel_id=1, source_target_pairs={{0,8},{4,12},{8,16},{12,20},{16,24},{20,28},{1,9},{5,13},{9,17},{1... | collective-permute-start | bytes 442376 | tf_op jit(solution)/shard_map/ppermute | solution.py:268
  18.9 1.5 %collective-permute-start.9 = (bf16[2,1024,256]{2,1,0:T(8,128)(2,1)}, bf16[2,1024,256]{2,1,0:T(8,128)(2,1)}, u32[]{:S(2)}, u32[]{:S(2)}) collective-permute-start(bf16[2,1024,256]{2,1,0:T(8,128)(2,1)} %pad_maximum_fusion.3), channel_id=1, source_target_pairs={{0,2},{1,3},{2,0},{3,1},{4,6},{5,7},{6,4},{7,5},{8,10},{9,11},{10,... | collective-permute-start | bytes 3145736 | tf_op jit(solution)/shard_map/ppermute | solution.py:252
  20.4 4.5 %collective-permute-start.7 = (bf16[9,64,128]{2,1,0:T(8,128)(2,1)}, bf16[9,64,128]{2,1,0:T(8,128)(2,1)S(1)}, u32[]{:S(2)}, u32[]{:S(2)}) collective-permute-start(bf16[9,64,128]{2,1,0:T(8,128)(2,1)} %collective-permute-done.6), channel_id=1, source_target_pairs={{0,8},{4,12},{8,16},{12,20},{16,24},{20,28},{1,9},{5,13},{9,17},{1... | collective-permute-start | bytes 442376 | tf_op jit(solution)/shard_map/ppermute | solution.py:268
  28.9 3.4 %collective-permute-done.5 = bf16[9,64,128]{2,1,0:T(8,128)(2,1)S(1)} collective-permute-done((bf16[9,64,128]{2,1,0:T(8,128)(2,1)}, bf16[9,64,128]{2,1,0:T(8,128)(2,1)S(1)}, u32[]{:S(2)}, u32[]{:S(2)}) %collective-permute-start.5) | collective-permute-done | bytes 147488 | tf_op jit(solution)/shard_map/ppermute | solution.py:269
  32.4 1.6 %collective-permute-start.8 = (bf16[4,9,64,128]{3,2,1,0:T(8,128)(2,1)S(1)}, bf16[4,9,64,128]{3,2,1,0:T(8,128)(2,1)S(1)}, u32[]{:S(2)}, u32[]{:S(2)}) collective-permute-start(bf16[4,9,64,128]{3,2,1,0:T(8,128)(2,1)S(1)} %get-tuple-element.31), channel_id=1, source_target_pairs={{0,4},{4,0},{8,12},{12,8},{16,20},{20,16},{24,28},{28,24},{1,5},{5... | collective-permute-start | bytes 1769480 | tf_op jit(solution)/shard_map/ppermute | solution.py:255
  33.9 2.8 %copy-done.8 = bf16[1024,3072]{1,0:T(8,128)(2,1)S(1)} copy-done((bf16[1024,3072]{1,0:T(8,128)(2,1)S(1)}, bf16[1024,3072]{1,0:T(8,128)(2,1)}, u32[]{:S(2)}) %copy-start.8) | copy-done | bytes 6291480
  36.7 4.3 %pack.1.packed = bf16[512,3072]{1,0:T(8,128)(2,1)S(1)} custom-call(bf16[512,1024]{1,0:T(8,128)(2,1)S(1)} %copy-done.10, bf16[1024,3072]{1,0:T(8,128)(2,1)S(1)} %copy-done.8), custom_call_target="tpu_custom_call" | custom-call | flops 3221225472 | bytes 10485760 | tf_op jit(solution)/shard_map/pack/pallas_call | solution.py:97
  41.1 8.0 %attend.1.refs_0_.refs_2_ = bf16[512,1024]{1,0:T(8,128)(2,1)S(1)} custom-call(s32[4]{0:T(128)S(1)} %copy-done.7, bf16[512,3072]{1,0:T(8,128)(2,1)S(1)} %pack.1.packed, bf16[512,1024]{1,0:T(8,128)(2,1)S(1)} %copy-done.11, bf16[1024,1024]{1,0:T(8,128)(2,1)S(1)} %copy-done.9, f32[1,1024]{1,0:T(1,128)S(1)} %bitcast.26), custom_call_target="tpu_custom_call" | custom-call | flops 3221225472 | bytes 8388608 | tf_op jit(solution)/shard_map/attend/pallas_call | solution.py:111
  49.8 1.7 %collective-permute-start.11 = (bf16[2,1024,256]{2,1,0:T(8,128)(2,1)}, bf16[2,1024,256]{2,1,0:T(8,128)(2,1)S(1)}, u32[]{:S(2)}, u32[]{:S(2)}) collective-permute-start(bf16[2,1024,256]{2,1,0:T(8,128)(2,1)} %get-tuple-element.22.refs_0_), channel_id=1, source_target_pairs={{0,8},{4,12},{8,0},{12,4},{16,24},{20,28},{24,16},{28,20},{1,9},{5... | collective-permute-start | bytes 3145736 | tf_op jit(solution)/shard_map/ppermute | solution.py:260
  52.1 2.9 %feed.6.refs_1_ = f32[512,1024]{1,0:T(8,128)S(1)} custom-call(bf16[512,1024]{1,0:T(8,128)(2,1)S(1)} %attend.1.refs_0_.refs_2_, bf16[1024,1024]{1,0:T(8,128)(2,1)S(1)} %copy-done.4, bf16[1024,1024]{1,0:T(8,128)(2,1)S(1)} %copy-done.5), custom_call_target="tpu_custom_call" | custom-call | flops 2147483648 | bytes 8388608 | tf_op jit(solution)/shard_map/feed/pallas_call | solution.py:176
  55.0 4.5 %feed.7.refs_3_.refs_1_ = f32[512,1024]{1,0:T(8,128)S(1)} custom-call(bf16[512,1024]{1,0:T(8,128)(2,1)S(1)} %attend.1.refs_0_.refs_2_, f32[512,1024]{1,0:T(8,128)S(1)} %feed.6.refs_1_, bf16[1024,1024]{1,0:T(8,128)(2,1)S(1)} %collective-permute-done.refs_2_, bf16[1024,1024]{1,0:T(8,128)(2,1)} %collective-permute-done.1.refs_3_), custom_call_target="tpu_custom_call" | custom-call | flops 2147483648 | bytes 8388608 | tf_op jit(solution)/shard_map/feed/pallas_call | solution.py:176
  59.5 13.0 %collective-permute-done.10.refs_1_ = bf16[2,1024,256]{2,1,0:T(8,128)(2,1)S(1)} collective-permute-done((bf16[2,1024,256]{2,1,0:T(8,128)(2,1)}, bf16[2,1024,256]{2,1,0:T(8,128)(2,1)S(1)}, u32[]{:S(2)}, u32[]{:S(2)}) %collective-permute-start.10) | collective-permute-done | bytes 1048608 | tf_op jit(solution)/shard_map/ppermute | solution.py:260
  73.6 1.8 %collective-permute-start.16 = (bf16[2,1024,128]{2,1,0:T(8,128)(2,1)S(1)}, bf16[2,1024,128]{2,1,0:T(8,128)(2,1)}, u32[]{:S(2)}, u32[]{:S(2)}) collective-permute-start(bf16[2,1024,128]{2,1,0:T(8,128)(2,1)S(1)} %slice.25), channel_id=1, source_target_pairs={{0,8},{4,12},{8,0},{12,4},{16,24},{20,28},{24,16},{28,20},{1,9},{5... | collective-permute-start | bytes 1572872 | tf_op jit(solution)/shard_map/ppermute | solution.py:260
  75.3 1.7 %collective-permute-done.15 = bf16[2,4,9,64,128]{4,3,2,1,0:T(8,128)(2,1)S(1)} collective-permute-done((bf16[2,4,9,64,128]{4,3,2,1,0:T(8,128)(2,1)S(1)}, bf16[2,4,9,64,128]{4,3,2,1,0:T(8,128)(2,1)S(1)}, u32[]{:S(2)}, u32[]{:S(2)}) %collective-permute-start.15) | collective-permute-done | bytes 1179680 | tf_op jit(solution)/shard_map/ppermute | solution.py:252
  77.0 1.5 %collective-permute-start.17 = (bf16[2,1024,128]{2,1,0:T(8,128)(2,1)S(1)}, bf16[2,1024,128]{2,1,0:T(8,128)(2,1)}, u32[]{:S(2)}, u32[]{:S(2)}) collective-permute-start(bf16[2,1024,128]{2,1,0:T(8,128)(2,1)S(1)} %slice.26), channel_id=1, source_target_pairs={{0,4},{4,0},{8,12},{12,8},{16,20},{20,16},{24,28},{28,24},{1,5},{5... | collective-permute-start | bytes 1572872 | tf_op jit(solution)/shard_map/ppermute | solution.py:260
  78.5 3.5 %feed.8.refs_1_ = f32[512,1024]{1,0:T(8,128)S(1)} custom-call(bf16[512,1024]{1,0:T(8,128)(2,1)S(1)} %attend.1.refs_0_.refs_2_, f32[512,1024]{1,0:T(8,128)S(1)} %feed.7.refs_3_.refs_1_, bf16[2,1024,256]{2,1,0:T(8,128)(2,1)} %get-tuple-element.23.refs_2_, bf16[2,1024,256]{2,1,0:T(8,128)(2,1)S(1)} %get-tuple-element.24.refs_3_, ...), custom_call_target="tpu_custom_call" | custom-call | flops 1610612736 | bytes 8388608 | tf_op jit(solution)/shard_map/feed/pallas_call | solution.py:176
  82.3 2.3 %feed.9.refs_3_.refs_1_ = f32[512,1024]{1,0:T(8,128)S(1)} custom-call(bf16[512,1024]{1,0:T(8,128)(2,1)S(1)} %attend.1.refs_0_.refs_2_, f32[512,1024]{1,0:T(8,128)S(1)} %feed.8.refs_1_, bf16[2,1024,256]{2,1,0:T(8,128)(2,1)S(1)} %collective-permute-done.12.refs_2_, bf16[2,1024,256]{2,1,0:T(8,128)(2,1)S(1)} %collective-permute-done.13.refs_3_, ...), custom_call_target="tpu_custom_call" | custom-call | flops 1610612736 | bytes 8388608 | tf_op jit(solution)/shard_map/feed/pallas_call | solution.py:176
  84.7 3.4 %collective-permute-done.16.refs_1_ = bf16[2,1024,128]{2,1,0:T(8,128)(2,1)} collective-permute-done((bf16[2,1024,128]{2,1,0:T(8,128)(2,1)S(1)}, bf16[2,1024,128]{2,1,0:T(8,128)(2,1)}, u32[]{:S(2)}, u32[]{:S(2)}) %collective-permute-start.16) | collective-permute-done | bytes 524320 | tf_op jit(solution)/shard_map/ppermute | solution.py:260
  90.3 1.6 %copy-done.1 = f32[512,1024]{1,0:T(8,128)S(1)} copy-done((f32[512,1024]{1,0:T(8,128)S(1)}, f32[512,1024]{1,0:T(8,128)}, u32[]{:S(2)}) %copy-start.1) | copy-done | bytes 2097176
  91.9 3.0 %feed.10.refs_4_ = f32[512,1024]{1,0:T(8,128)S(1)} custom-call(bf16[512,1024]{1,0:T(8,128)(2,1)S(1)} %attend.1.refs_0_.refs_2_, f32[512,1024]{1,0:T(8,128)S(1)} %copy-done.1, bf16[2,1024,128]{2,1,0:T(8,128)(2,1)} %get-tuple-element.27.refs_2_, bf16[2,1024,128]{2,1,0:T(8,128)(2,1)} %get-tuple-element.28.refs_3_), custom_call_target="tpu_custom_call" | custom-call | flops 536870912 | bytes 8388608 | tf_op jit(solution)/shard_map/feed/pallas_call | solution.py:176
  95.5 4.8 %feed.11.embedded_ref = bf16[512,128]{1,0:T(8,128)(2,1)} custom-call(bf16[512,1024]{1,0:T(8,128)(2,1)S(1)} %attend.1.refs_0_.refs_2_, s32[4]{0:T(128)S(1)} %copy-done.7, f32[1,1024]{1,0:T(1,128)S(1)} %bitcast.25, bf16[1024,128]{1,0:T(8,128)(2,1)S(1)} %copy-done.3, f32[512,1024]{1,0:T(8,128)S(1)} %feed.10.refs_4_, ...), custom_call_target="tpu_custom_call" | custom-call | flops 536870912 | bytes 8388608 | tf_op jit(solution)/shard_map/feed/pallas_call | solution.py:176
  100.3 2.1 %pad_maximum_fusion = bf16[2,2,2,4,9,64,128]{6,5,4,3,2,1,0:T(8,128)(2,1)S(1)} fusion(bf16[1,2,2,4,9,64,128]{6,5,4,3,2,1,0:T(8,128)(2,1)} %bitcast.13, bf16[1,2,2,4,9,64,128]{6,5,4,3,2,1,0:T(8,128)(2,1)S(1)} %bitcast.22), kind=kLoop, calls=%fused_computation | loop fusion | flops 2359296 | bytes 9437184 | tf_op jit(solution)/shard_map/stack | solution.py:310
  102.5 2.1 %score.1 = f32[4,8,128]{2,1,0:T(8,128)S(1)} custom-call(s32[4,8,4]{2,1,0:T(8,128)S(1)} %get-tuple-element.35.spots_ref, s32[4,8]{1,0:T(4,128)S(1)} %fusion.marks_ref, s32[4,8]{1,0:T(4,128)S(1)} %get-tuple-element.38.rows_ref, bf16[512,128]{1,0:T(8,128)(2,1)S(1)} %copy-done.2, bf16[288,64,128]{2,1,0:T(8,128)(2,1)S(1)} %bitcast.23), custom_call_target="tpu_custom_call" | custom-call | flops 268435456 | bytes 5242880 | tf_op jit(solution)/shard_map/score/pallas_call | solution.py:214
  (79 shorter events, 18.2 us)
Async XLA Ops:
  2.3 8.0 %collective-permute-start.2 = (bf16[9,64,128]{2,1,0:T(8,128)(2,1)S(1)}, bf16[9,64,128]{2,1,0:T(8,128)(2,1)S(1)}, u32[]{:S(2)}, u32[]{:S(2)}) collective-permute-start(bf16[9,64,128]{2,1,0:T(8,128)(2,1)S(1)} %get-tuple-element.33), channel_id=1, source_target_pairs={{0,8},{4,12},{8,16},{12,20},{16,24},{20,28},{1,9},{5,13},{9,17},{1... | collective-permute-start | bytes 442376 | tf_op jit(solution)/shard_map/ppermute | solution.py:268
  7.2 8.2 %collective-permute-start.3 = (bf16[9,64,128]{2,1,0:T(8,128)(2,1)S(1)}, bf16[9,64,128]{2,1,0:T(8,128)(2,1)}, u32[]{:S(2)}, u32[]{:S(2)}) collective-permute-start(bf16[9,64,128]{2,1,0:T(8,128)(2,1)S(1)} %get-tuple-element.33), channel_id=1, source_target_pairs={{8,0},{12,4},{16,8},{20,12},{24,16},{28,20},{9,1},{13,5},{17,9},{2... | collective-permute-start | bytes 442376 | tf_op jit(solution)/shard_map/ppermute | solution.py:269
  8.6 46.4 %collective-permute-start = (bf16[1024,1024]{1,0:T(8,128)(2,1)}, bf16[1024,1024]{1,0:T(8,128)(2,1)S(1)}, u32[]{:S(2)}, u32[]{:S(2)}) collective-permute-start(bf16[1024,1024]{1,0:T(8,128)(2,1)} %refs_1_.2), channel_id=1, source_target_pairs={{0,1},{1,0},{2,3},{3,2},{4,5},{5,4},{6,7},{7,6},{8,9},{9,8},{10,11... | collective-permute-start | bytes 6291464 | tf_op jit(solution)/shard_map/ppermute | solution.py:249
  8.6 46.4 %collective-permute-start.1 = (bf16[1024,1024]{1,0:T(8,128)(2,1)}, bf16[1024,1024]{1,0:T(8,128)(2,1)}, u32[]{:S(2)}, u32[]{:S(2)}) collective-permute-start(bf16[1024,1024]{1,0:T(8,128)(2,1)} %refs_2_.1), channel_id=1, source_target_pairs={{0,1},{1,0},{2,3},{3,2},{4,5},{5,4},{6,7},{7,6},{8,9},{9,8},{10,11... | collective-permute-start | bytes 6291464 | tf_op jit(solution)/shard_map/ppermute | solution.py:249
  10.3 10.1 %collective-permute-start.6 = (bf16[9,64,128]{2,1,0:T(8,128)(2,1)S(1)}, bf16[9,64,128]{2,1,0:T(8,128)(2,1)}, u32[]{:S(2)}, u32[]{:S(2)}) collective-permute-start(bf16[9,64,128]{2,1,0:T(8,128)(2,1)S(1)} %collective-permute-done.2), channel_id=1, source_target_pairs={{0,8},{4,12},{8,16},{12,20},{16,24},{20,28},{1,9},{5,13},{9,17},{1... | collective-permute-start | bytes 442376 | tf_op jit(solution)/shard_map/ppermute | solution.py:268
  15.4 9.5 %collective-permute-start.4 = (bf16[9,64,128]{2,1,0:T(8,128)(2,1)}, bf16[9,64,128]{2,1,0:T(8,128)(2,1)}, u32[]{:S(2)}, u32[]{:S(2)}) collective-permute-start(bf16[9,64,128]{2,1,0:T(8,128)(2,1)} %collective-permute-done.3), channel_id=1, source_target_pairs={{8,0},{12,4},{16,8},{20,12},{24,16},{28,20},{9,1},{13,5},{17,9},{2... | collective-permute-start | bytes 442376 | tf_op jit(solution)/shard_map/ppermute | solution.py:269
  17.8 16.1 %copy-start.10 = (bf16[512,1024]{1,0:T(8,128)(2,1)S(1)}, bf16[512,1024]{1,0:T(8,128)(2,1)}, u32[]{:S(2)}) copy-start(bf16[512,1024]{1,0:T(8,128)(2,1)} %tokens_ref.3) | copy-start | bytes 3145732
  18.9 30.3 %collective-permute-start.9 = (bf16[2,1024,256]{2,1,0:T(8,128)(2,1)}, bf16[2,1024,256]{2,1,0:T(8,128)(2,1)}, u32[]{:S(2)}, u32[]{:S(2)}) collective-permute-start(bf16[2,1024,256]{2,1,0:T(8,128)(2,1)} %pad_maximum_fusion.3), channel_id=1, source_target_pairs={{0,2},{1,3},{2,0},{3,1},{4,6},{5,7},{6,4},{7,5},{8,10},{9,11},{10,... | collective-permute-start | bytes 3145736 | tf_op jit(solution)/shard_map/ppermute | solution.py:252
  20.4 7.5 %collective-permute-start.7 = (bf16[9,64,128]{2,1,0:T(8,128)(2,1)}, bf16[9,64,128]{2,1,0:T(8,128)(2,1)S(1)}, u32[]{:S(2)}, u32[]{:S(2)}) collective-permute-start(bf16[9,64,128]{2,1,0:T(8,128)(2,1)} %collective-permute-done.6), channel_id=1, source_target_pairs={{0,8},{4,12},{8,16},{12,20},{16,24},{20,28},{1,9},{5,13},{9,17},{1... | collective-permute-start | bytes 442376 | tf_op jit(solution)/shard_map/ppermute | solution.py:268
  25.0 7.2 %collective-permute-start.5 = (bf16[9,64,128]{2,1,0:T(8,128)(2,1)}, bf16[9,64,128]{2,1,0:T(8,128)(2,1)S(1)}, u32[]{:S(2)}, u32[]{:S(2)}) collective-permute-start(bf16[9,64,128]{2,1,0:T(8,128)(2,1)} %collective-permute-done.4), channel_id=1, source_target_pairs={{8,0},{12,4},{16,8},{20,12},{24,16},{28,20},{9,1},{13,5},{17,9},{2... | collective-permute-start | bytes 442376 | tf_op jit(solution)/shard_map/ppermute | solution.py:269
  32.4 8.7 %copy-start.7 = (s32[4]{0:T(128)S(1)}, s32[4]{0:T(128)}, u32[]{:S(2)}) copy-start(s32[4]{0:T(128)} %refs_1_.3) | copy-start | bytes 52
  32.4 16.7 %collective-permute-start.8 = (bf16[4,9,64,128]{3,2,1,0:T(8,128)(2,1)S(1)}, bf16[4,9,64,128]{3,2,1,0:T(8,128)(2,1)S(1)}, u32[]{:S(2)}, u32[]{:S(2)}) collective-permute-start(bf16[4,9,64,128]{3,2,1,0:T(8,128)(2,1)S(1)} %get-tuple-element.31), channel_id=1, source_target_pairs={{0,4},{4,0},{8,12},{12,8},{16,20},{20,16},{24,28},{28,24},{1,5},{5... | collective-permute-start | bytes 1769480 | tf_op jit(solution)/shard_map/ppermute | solution.py:255
  49.2 23.3 %collective-permute-start.10 = (bf16[2,1024,256]{2,1,0:T(8,128)(2,1)}, bf16[2,1024,256]{2,1,0:T(8,128)(2,1)S(1)}, u32[]{:S(2)}, u32[]{:S(2)}) collective-permute-start(bf16[2,1024,256]{2,1,0:T(8,128)(2,1)} %get-tuple-element.22.refs_0_), channel_id=1, source_target_pairs={{0,4},{4,0},{8,12},{12,8},{16,20},{20,16},{24,28},{28,24},{1,5},{5... | collective-permute-start | bytes 3145736 | tf_op jit(solution)/shard_map/ppermute | solution.py:260
  49.8 23.1 %collective-permute-start.11 = (bf16[2,1024,256]{2,1,0:T(8,128)(2,1)}, bf16[2,1024,256]{2,1,0:T(8,128)(2,1)S(1)}, u32[]{:S(2)}, u32[]{:S(2)}) collective-permute-start(bf16[2,1024,256]{2,1,0:T(8,128)(2,1)} %get-tuple-element.22.refs_0_), channel_id=1, source_target_pairs={{0,8},{4,12},{8,0},{12,4},{16,24},{20,28},{24,16},{28,20},{1,9},{5... | collective-permute-start | bytes 3145736 | tf_op jit(solution)/shard_map/ppermute | solution.py:260
  51.6 25.4 %collective-permute-start.15 = (bf16[2,4,9,64,128]{4,3,2,1,0:T(8,128)(2,1)S(1)}, bf16[2,4,9,64,128]{4,3,2,1,0:T(8,128)(2,1)S(1)}, u32[]{:S(2)}, u32[]{:S(2)}) collective-permute-start(bf16[2,4,9,64,128]{4,3,2,1,0:T(8,128)(2,1)S(1)} %get-tuple-element.26), channel_id=1, source_target_pairs={{0,2},{1,3},{2,0},{3,1},{4,6},{5,7},{6,4},{7,5},{8,10},{9,11},{10,... | collective-permute-start | bytes 3538952 | tf_op jit(solution)/shard_map/ppermute | solution.py:252
  73.0 9.3 %collective-permute-start.12 = (bf16[2,1024,256]{2,1,0:T(8,128)(2,1)}, bf16[2,1024,256]{2,1,0:T(8,128)(2,1)S(1)}, u32[]{:S(2)}, u32[]{:S(2)}) collective-permute-start(bf16[2,1024,256]{2,1,0:T(8,128)(2,1)} %get-tuple-element.23.refs_2_), channel_id=1, source_target_pairs={{0,1},{1,0},{2,3},{3,2},{4,5},{5,4},{6,7},{7,6},{8,9},{9,8},{10,11... | collective-permute-start | bytes 3145736 | tf_op jit(solution)/shard_map/ppermute | solution.py:249
  73.0 9.3 %collective-permute-start.13 = (bf16[2,1024,256]{2,1,0:T(8,128)(2,1)S(1)}, bf16[2,1024,256]{2,1,0:T(8,128)(2,1)S(1)}, u32[]{:S(2)}, u32[]{:S(2)}) collective-permute-start(bf16[2,1024,256]{2,1,0:T(8,128)(2,1)S(1)} %get-tuple-element.24.refs_3_), channel_id=1, source_target_pairs={{0,1},{1,0},{2,3},{3,2},{4,5},{5,4},{6,7},{7,6},{8,9},{9,8},{10,11... | collective-permute-start | bytes 3145736 | tf_op jit(solution)/shard_map/ppermute | solution.py:249
  73.5 8.8 %collective-permute-start.14 = (bf16[2,1024,256]{2,1,0:T(8,128)(2,1)S(1)}, bf16[2,1024,256]{2,1,0:T(8,128)(2,1)S(1)}, u32[]{:S(2)}, u32[]{:S(2)}) collective-permute-start(bf16[2,1024,256]{2,1,0:T(8,128)(2,1)S(1)} %get-tuple-element.25.refs_4_), channel_id=1, source_target_pairs={{0,1},{1,0},{2,3},{3,2},{4,5},{5,4},{6,7},{7,6},{8,9},{9,8},{10,11... | collective-permute-start | bytes 3145736 | tf_op jit(solution)/shard_map/ppermute | solution.py:249
  73.6 14.5 %collective-permute-start.16 = (bf16[2,1024,128]{2,1,0:T(8,128)(2,1)S(1)}, bf16[2,1024,128]{2,1,0:T(8,128)(2,1)}, u32[]{:S(2)}, u32[]{:S(2)}) collective-permute-start(bf16[2,1024,128]{2,1,0:T(8,128)(2,1)S(1)} %slice.25), channel_id=1, source_target_pairs={{0,8},{4,12},{8,0},{12,4},{16,24},{20,28},{24,16},{28,20},{1,9},{5... | collective-permute-start | bytes 1572872 | tf_op jit(solution)/shard_map/ppermute | solution.py:260
  77.0 12.5 %collective-permute-start.17 = (bf16[2,1024,128]{2,1,0:T(8,128)(2,1)S(1)}, bf16[2,1024,128]{2,1,0:T(8,128)(2,1)}, u32[]{:S(2)}, u32[]{:S(2)}) collective-permute-start(bf16[2,1024,128]{2,1,0:T(8,128)(2,1)S(1)} %slice.26), channel_id=1, source_target_pairs={{0,4},{4,0},{8,12},{12,8},{16,20},{20,16},{24,28},{28,24},{1,5},{5... | collective-permute-start | bytes 1572872 | tf_op jit(solution)/shard_map/ppermute | solution.py:260
  84.6 5.4 %copy-start.13 = (s32[4,8]{1,0:T(4,128)S(1)}, s32[4,8]{1,0:T(4,128)}, u32[]{:S(2)}) copy-start(s32[4,8]{1,0:T(4,128)} %param.25) | copy-start | bytes 388
  89.5 10.8 %collective-permute-start.20 = (bf16[2,2,4,9,64,128]{5,4,3,2,1,0:T(8,128)(2,1)S(1)}, bf16[2,2,4,9,64,128]{5,4,3,2,1,0:T(8,128)(2,1)}, u32[]{:S(2)}, u32[]{:S(2)}) collective-permute-start(bf16[2,2,4,9,64,128]{5,4,3,2,1,0:T(8,128)(2,1)S(1)} %get-tuple-element.29), channel_id=1, source_target_pairs={{0,1},{1,0},{2,3},{3,2},{4,5},{5,4},{6,7},{7,6},{8,9},{9,8},{10,11... | collective-permute-start | bytes 7077896 | tf_op jit(solution)/shard_map/ppermute | solution.py:249
  89.5 5.4 %collective-permute-start.18 = (bf16[2,1024,128]{2,1,0:T(8,128)(2,1)}, bf16[2,1024,128]{2,1,0:T(8,128)(2,1)}, u32[]{:S(2)}, u32[]{:S(2)}) collective-permute-start(bf16[2,1024,128]{2,1,0:T(8,128)(2,1)} %get-tuple-element.27.refs_2_), channel_id=1, source_target_pairs={{0,1},{1,0},{2,3},{3,2},{4,5},{5,4},{6,7},{7,6},{8,9},{9,8},{10,11... | collective-permute-start | bytes 1572872 | tf_op jit(solution)/shard_map/ppermute | solution.py:249
  90.0 5.5 %collective-permute-start.19 = (bf16[2,1024,128]{2,1,0:T(8,128)(2,1)}, bf16[2,1024,128]{2,1,0:T(8,128)(2,1)}, u32[]{:S(2)}, u32[]{:S(2)}) collective-permute-start(bf16[2,1024,128]{2,1,0:T(8,128)(2,1)} %get-tuple-element.28.refs_3_), channel_id=1, source_target_pairs={{0,1},{1,0},{2,3},{3,2},{4,5},{5,4},{6,7},{7,6},{8,9},{9,8},{10,11... | collective-permute-start | bytes 1572872 | tf_op jit(solution)/shard_map/ppermute | solution.py:249
  (11 other events, 37.4 us)

commit v3 on v2

--- a/solution.py
+++ b/solution.py
@@ -263,13 +263,10 @@
     listed = listed.at[:held_docs].set(document_length.astype(jnp.bfloat16)[:, None])
     block = jnp.concatenate([documents, listed[None]], axis=0)
     held = held_docs + 1
-    upward, downward = [block], [block]
-    for _ in range(1, DEPTH):
-        upward.append(lax.ppermute(upward[-1], "req", [(r, r + width) for r in range(req_size - width)]))
-        downward.append(lax.ppermute(downward[-1], "req", [(r, r - width) for r in range(width, req_size)]))
-    around = jnp.stack(
-        [block] + [jnp.where(z >= hop, upward[hop], downward[DEPTH - hop]) for hop in range(1, DEPTH)]
-    )
+    around = jnp.stack([block, to_pair(block, width)])
+    around = jnp.stack([around, to_pair(around, 2 * width)]).reshape(DEPTH, *block.shape)
+    packed = pack(tokens, attend_weight, [])
+    around = gate([around], [packed])[0]
     from_x = [along_x(around, hop) for hop in range(1, width)]
 
     place = x % 2 + 2 * (z % 2)
@@ -285,7 +282,6 @@
     partner = [to_core(up_weight), to_core(down_weight)]
 
 
-    packed = pack(tokens, attend_weight, [])
     normed = attend(packed, tokens, output_weight, attend_gain, query_length, [])
     around = jnp.stack([around] + from_x)
     held_back = gate([around] + firsts, [normed])
@@ -315,7 +311,7 @@
 
     owner = candidates // held_docs
     parts = jnp.arange(mlp_size, dtype=jnp.int32)
-    away_z = (z - owner // width) % DEPTH
+    away_z = z ^ (owner // width)
     away_x = (x - owner % width) % width
     away_y = (y - parts // CORES) % tall
     away_core = (core + parts) % CORES

time: 106 us -> 98.5 us (0.929)
  starting transfers between devices: 29.2 us -> 17.3 us
  waiting for transfers between devices: 24.8 us -> 33.4 us
  other arithmetic: 8.03 us -> 5.17 us
  Pallas kernels: 35.4 us -> 34.2 us
    ppermute x6 -> x0, starting transfers between devices: 18.4 us -> none  [the longest x3 14.6 us: on_device(): lax.ppermute(upward[-1], 'req', [(r, r + width) for r in range(req_size -...]
    ppermute x4 -> x6, waiting for transfers between devices: 18.4 us -> 26.1 us  [to_pair(): lax.ppermute(block, 'req', [(r, r ^ stride) for r in range(req_size)])]
    ppermute x4 -> x6, starting transfers between devices: 5.59 us -> 11.2 us  [to_pair(): lax.ppermute(block, 'req', [(r, r ^ stride) for r in range(req_size)])]
    ppermute x1, waiting for transfers between devices: 0.01 us -> 4.83 us  [along_x(): lax.ppermute(block, 'req', [(r, r // width * width + (r % width + hops) %...]
    ppermute x6 -> x0, waiting for transfers between devices: 4.2 us -> none  [the longest x3 3.37 us: on_device(): lax.ppermute(downward[-1], 'req', [(r, r - width) for r in range(width, r...]
    another operation x4 -> x3, other arithmetic: 2.81 us -> 1.02 us  [the longest x1 0.93 us: on_device(): around = jnp.stack([block, to_pair(block, width)])]
    pallas_call x6, Pallas kernels: 21 us -> 19.8 us  [feed(): pl.pallas_call(functools.partial(feed_kernel, weights[0].ndim, ending is...]
    ppermute x2, starting transfers between devices: 2.02 us -> 3.1 us  [along_y(): lax.ppermute(block, 'mlp', [(m, (m + CORES * hops) % mlp_size) for m in r...]
  transfers between devices with their start and end apart: 21 -> 17, of which waited for: 9 -> 9; matrix products, arithmetic and copies ran while one was open for 6% -> 5% of each run, Pallas kernels for 32% -> 33%
where the time goes in v3:
time: 98.5 us; the launch traced here: 98 us
  Pallas kernels  34.2 us (35%)
  waiting for transfers between devices  33.4 us (34%)
  starting transfers between devices  17.3 us (18%)
  local copies, waits for them, and re-layouts  6.99 us (7%)
  other arithmetic  5.17 us (5%)
    ppermute x6, waiting for transfers between devices, to_pair(): lax.ppermute(block, 'req', [(r, r ^ stride) for r in range(req_size)])  26.1 us
    pallas_call x6, Pallas kernels, feed(): pl.pallas_call(functools.partial(feed_kernel, weights[0].ndim, ending is...  19.8 us
    ppermute x6, starting transfers between devices, to_pair(): lax.ppermute(block, 'req', [(r, r ^ stride) for r in range(req_size)])  11.2 us
    pallas_call x1, Pallas kernels, attend(): pl.pallas_call(attend_kernel, out_shape=jax.ShapeDtypeStruct((rows, D), j...  8 us
    ppermute x1, waiting for transfers between devices, along_x(): lax.ppermute(block, 'req', [(r, r // width * width + (r % width + hops) %...  4.83 us
    unnamed x26, local copies, waits for them, and re-layouts  4.59 us
    pallas_call x1, Pallas kernels, pack(): pl.pallas_call(pack_kernel, out_shape=jax.ShapeDtypeStruct((rows, 3 * D),...  4.29 us
    ppermute x2, starting transfers between devices, along_y(): lax.ppermute(block, 'mlp', [(m, (m + CORES * hops) % mlp_size) for m in r...  3.1 us
  transfers between devices with their start and end apart: 17, of which 9 were waited for; matrix products, arithmetic and copies ran while one was open for 5% of the time, Pallas kernels for 33%

profile of v3, /device:TPU:0, one launch (start us, length us, event | category | flops | bytes accessed | tf_op | source)
XLA Modules:
  0.0 98.0 jit_solution(4135815674966405510)
XLA Ops:
  2.9 3.1 %collective-permute-start.2 = (bf16[9,64,128]{2,1,0:T(8,128)(2,1)S(1)}, bf16[9,64,128]{2,1,0:T(8,128)(2,1)S(1)}, u32[]{:S(2)}, u32[]{:S(2)}) collective-permute-start(bf16[9,64,128]{2,1,0:T(8,128)(2,1)S(1)} %get-tuple-element.33), channel_id=1, source_target_pairs={{0,8},{4,12},{8,0},{12,4},{16,24},{20,28},{24,16},{28,20},{1,9},{5... | collective-permute-start | bytes 442376 | tf_op jit(solution)/shard_map/ppermute | solution.py:260
  8.3 1.6 %collective-permute-start.5 = (bf16[2,1024,256]{2,1,0:T(8,128)(2,1)S(1)}, bf16[2,1024,256]{2,1,0:T(8,128)(2,1)S(1)}, u32[]{:S(2)}, u32[]{:S(2)}) collective-permute-start(bf16[2,1024,256]{2,1,0:T(8,128)(2,1)S(1)} %pad_maximum_fusion.3), channel_id=1, source_target_pairs={{0,2},{1,3},{2,0},{3,1},{4,6},{5,7},{6,4},{7,5},{8,10},{9,11},{10,... | collective-permute-start | bytes 3145736 | tf_op jit(solution)/shard_map/ppermute | solution.py:252
  10.1 2.8 %collective-permute-start.3 = (bf16[2,9,64,128]{3,2,1,0:T(8,128)(2,1)S(1)}, bf16[2,9,64,128]{3,2,1,0:T(8,128)(2,1)S(1)}, u32[]{:S(2)}, u32[]{:S(2)}) collective-permute-start(bf16[2,9,64,128]{3,2,1,0:T(8,128)(2,1)S(1)} %get-tuple-element.31), channel_id=1, source_target_pairs={{0,16},{4,20},{8,24},{12,28},{16,0},{20,4},{24,8},{28,12},{1,17},{... | collective-permute-start | bytes 884744 | tf_op jit(solution)/shard_map/ppermute | solution.py:260
  12.9 2.8 %copy-done.8 = bf16[1024,3072]{1,0:T(8,128)(2,1)S(1)} copy-done((bf16[1024,3072]{1,0:T(8,128)(2,1)S(1)}, bf16[1024,3072]{1,0:T(8,128)(2,1)}, u32[]{:S(2)}) %copy-start.8) | copy-done | bytes 6291480
  15.7 4.3 %pack.1.packed.refs_1_ = bf16[512,3072]{1,0:T(8,128)(2,1)S(1)} custom-call(bf16[512,1024]{1,0:T(8,128)(2,1)S(1)} %copy-done.10, bf16[1024,3072]{1,0:T(8,128)(2,1)S(1)} %copy-done.8), custom_call_target="tpu_custom_call" | custom-call | flops 3221225472 | bytes 10485760 | tf_op jit(solution)/shard_map/pack/pallas_call | solution.py:97
  20.0 5.8 %collective-permute-done.3 = bf16[2,9,64,128]{3,2,1,0:T(8,128)(2,1)S(1)} collective-permute-done((bf16[2,9,64,128]{3,2,1,0:T(8,128)(2,1)S(1)}, bf16[2,9,64,128]{3,2,1,0:T(8,128)(2,1)S(1)}, u32[]{:S(2)}, u32[]{:S(2)}) %collective-permute-start.3) | collective-permute-done | bytes 294944 | tf_op jit(solution)/shard_map/ppermute | solution.py:260
  27.5 8.0 %attend.1.refs_0_.refs_2_ = bf16[512,1024]{1,0:T(8,128)(2,1)S(1)} custom-call(s32[4]{0:T(128)S(1)} %copy-done.7, bf16[512,3072]{1,0:T(8,128)(2,1)S(1)} %pack.1.packed.refs_1_, bf16[512,1024]{1,0:T(8,128)(2,1)S(1)} %copy-done.10, bf16[1024,1024]{1,0:T(8,128)(2,1)S(1)} %copy-done.9, f32[1,1024]{1,0:T(1,128)S(1)} %bitcast.26), custom_call_target="tpu_custom_call" | custom-call | flops 3221225472 | bytes 8388608 | tf_op jit(solution)/shard_map/attend/pallas_call | solution.py:111
  35.5 4.8 %collective-permute-done.4 = bf16[4,9,64,128]{3,2,1,0:T(8,128)(2,1)S(1)} collective-permute-done((bf16[4,9,64,128]{3,2,1,0:T(8,128)(2,1)S(1)}, bf16[4,9,64,128]{3,2,1,0:T(8,128)(2,1)S(1)}, u32[]{:S(2)}, u32[]{:S(2)}) %collective-permute-start.4) | collective-permute-done | bytes 589856 | tf_op jit(solution)/shard_map/ppermute | solution.py:255
  41.8 1.8 %collective-permute-start.7 = (bf16[2,1024,256]{2,1,0:T(8,128)(2,1)S(1)}, bf16[2,1024,256]{2,1,0:T(8,128)(2,1)S(1)}, u32[]{:S(2)}, u32[]{:S(2)}) collective-permute-start(bf16[2,1024,256]{2,1,0:T(8,128)(2,1)S(1)} %get-tuple-element.22.refs_0_), channel_id=1, source_target_pairs={{0,8},{4,12},{8,0},{12,4},{16,24},{20,28},{24,16},{28,20},{1,9},{5... | collective-permute-start | bytes 3145736 | tf_op jit(solution)/shard_map/ppermute | solution.py:260
  43.5 1.5 %collective-permute-start.11 = (bf16[2,4,9,64,128]{4,3,2,1,0:T(8,128)(2,1)S(1)}, bf16[2,4,9,64,128]{4,3,2,1,0:T(8,128)(2,1)S(1)}, u32[]{:S(2)}, u32[]{:S(2)}) collective-permute-start(bf16[2,4,9,64,128]{4,3,2,1,0:T(8,128)(2,1)S(1)} %get-tuple-element.26), channel_id=1, source_target_pairs={{0,2},{1,3},{2,0},{3,1},{4,6},{5,7},{6,4},{7,5},{8,10},{9,11},{10,... | collective-permute-start | bytes 3538952 | tf_op jit(solution)/shard_map/ppermute | solution.py:252
  45.0 2.9 %feed.6.refs_1_ = f32[512,1024]{1,0:T(8,128)S(1)} custom-call(bf16[512,1024]{1,0:T(8,128)(2,1)S(1)} %attend.1.refs_0_.refs_2_, bf16[1024,1024]{1,0:T(8,128)(2,1)S(1)} %copy-done.4, bf16[1024,1024]{1,0:T(8,128)(2,1)S(1)} %copy-done.5), custom_call_target="tpu_custom_call" | custom-call | flops 2147483648 | bytes 8388608 | tf_op jit(solution)/shard_map/feed/pallas_call | solution.py:176
  48.0 4.5 %feed.7.refs_3_.refs_1_ = f32[512,1024]{1,0:T(8,128)S(1)} custom-call(bf16[512,1024]{1,0:T(8,128)(2,1)S(1)} %attend.1.refs_0_.refs_2_, f32[512,1024]{1,0:T(8,128)S(1)} %feed.6.refs_1_, bf16[1024,1024]{1,0:T(8,128)(2,1)S(1)} %collective-permute-done.refs_2_, bf16[1024,1024]{1,0:T(8,128)(2,1)} %collective-permute-done.1.refs_3_), custom_call_target="tpu_custom_call" | custom-call | flops 2147483648 | bytes 8388608 | tf_op jit(solution)/shard_map/feed/pallas_call | solution.py:176
  52.4 11.4 %collective-permute-done.6.refs_1_ = bf16[2,1024,256]{2,1,0:T(8,128)(2,1)S(1)} collective-permute-done((bf16[2,1024,256]{2,1,0:T(8,128)(2,1)S(1)}, bf16[2,1024,256]{2,1,0:T(8,128)(2,1)S(1)}, u32[]{:S(2)}, u32[]{:S(2)}) %collective-permute-start.6) | collective-permute-done | bytes 1048608 | tf_op jit(solution)/shard_map/ppermute | solution.py:260
  63.8 1.9 %collective-permute-done.7.refs_2_ = bf16[2,1024,256]{2,1,0:T(8,128)(2,1)S(1)} collective-permute-done((bf16[2,1024,256]{2,1,0:T(8,128)(2,1)S(1)}, bf16[2,1024,256]{2,1,0:T(8,128)(2,1)S(1)}, u32[]{:S(2)}, u32[]{:S(2)}) %collective-permute-start.7) | collective-permute-done | bytes 1048608 | tf_op jit(solution)/shard_map/ppermute | solution.py:260
  66.3 1.8 %collective-permute-start.12 = (bf16[2,1024,128]{2,1,0:T(8,128)(2,1)S(1)}, bf16[2,1024,128]{2,1,0:T(8,128)(2,1)}, u32[]{:S(2)}, u32[]{:S(2)}) collective-permute-start(bf16[2,1024,128]{2,1,0:T(8,128)(2,1)S(1)} %slice.25), channel_id=1, source_target_pairs={{0,8},{4,12},{8,0},{12,4},{16,24},{20,28},{24,16},{28,20},{1,9},{5... | collective-permute-start | bytes 1572872 | tf_op jit(solution)/shard_map/ppermute | solution.py:260
  68.1 1.9 %collective-permute-done.11 = bf16[2,4,9,64,128]{4,3,2,1,0:T(8,128)(2,1)S(1)} collective-permute-done((bf16[2,4,9,64,128]{4,3,2,1,0:T(8,128)(2,1)S(1)}, bf16[2,4,9,64,128]{4,3,2,1,0:T(8,128)(2,1)S(1)}, u32[]{:S(2)}, u32[]{:S(2)}) %collective-permute-start.11) | collective-permute-done | bytes 1179680 | tf_op jit(solution)/shard_map/ppermute | solution.py:252
  70.5 2.3 %feed.8.refs_1_ = f32[512,1024]{1,0:T(8,128)S(1)} custom-call(bf16[512,1024]{1,0:T(8,128)(2,1)S(1)} %attend.1.refs_0_.refs_2_, f32[512,1024]{1,0:T(8,128)S(1)} %feed.7.refs_3_.refs_1_, bf16[2,1024,256]{2,1,0:T(8,128)(2,1)S(1)} %get-tuple-element.23.refs_2_, bf16[2,1024,256]{2,1,0:T(8,128)(2,1)S(1)} %get-tuple-element.24.refs_3_, ...), custom_call_target="tpu_custom_call" | custom-call | flops 1610612736 | bytes 8388608 | tf_op jit(solution)/shard_map/feed/pallas_call | solution.py:176
  73.1 2.3 %feed.9.refs_3_.refs_1_ = f32[512,1024]{1,0:T(8,128)S(1)} custom-call(bf16[512,1024]{1,0:T(8,128)(2,1)S(1)} %attend.1.refs_0_.refs_2_, f32[512,1024]{1,0:T(8,128)S(1)} %feed.8.refs_1_, bf16[2,1024,256]{2,1,0:T(8,128)(2,1)S(1)} %collective-permute-done.8.refs_2_, bf16[2,1024,256]{2,1,0:T(8,128)(2,1)S(1)} %collective-permute-done.9.refs_3_, ...), custom_call_target="tpu_custom_call" | custom-call | flops 1610612736 | bytes 8388608 | tf_op jit(solution)/shard_map/feed/pallas_call | solution.py:176
  75.5 5.4 %collective-permute-done.12.refs_1_ = bf16[2,1024,128]{2,1,0:T(8,128)(2,1)} collective-permute-done((bf16[2,1024,128]{2,1,0:T(8,128)(2,1)S(1)}, bf16[2,1024,128]{2,1,0:T(8,128)(2,1)}, u32[]{:S(2)}, u32[]{:S(2)}) %collective-permute-start.12) | collective-permute-done | bytes 524320 | tf_op jit(solution)/shard_map/ppermute | solution.py:260
  83.1 1.6 %copy-done.1 = f32[512,1024]{1,0:T(8,128)S(1)} copy-done((f32[512,1024]{1,0:T(8,128)S(1)}, f32[512,1024]{1,0:T(8,128)}, u32[]{:S(2)}) %copy-start.1) | copy-done | bytes 2097176
  84.7 3.0 %feed.10.refs_4_ = f32[512,1024]{1,0:T(8,128)S(1)} custom-call(bf16[512,1024]{1,0:T(8,128)(2,1)S(1)} %attend.1.refs_0_.refs_2_, f32[512,1024]{1,0:T(8,128)S(1)} %copy-done.1, bf16[2,1024,128]{2,1,0:T(8,128)(2,1)} %get-tuple-element.27.refs_2_, bf16[2,1024,128]{2,1,0:T(8,128)(2,1)} %get-tuple-element.28.refs_3_), custom_call_target="tpu_custom_call" | custom-call | flops 536870912 | bytes 8388608 | tf_op jit(solution)/shard_map/feed/pallas_call | solution.py:176
  88.3 4.8 %feed.11.embedded_ref = bf16[512,128]{1,0:T(8,128)(2,1)} custom-call(bf16[512,1024]{1,0:T(8,128)(2,1)S(1)} %attend.1.refs_0_.refs_2_, s32[4]{0:T(128)S(1)} %copy-done.7, f32[1,1024]{1,0:T(1,128)S(1)} %bitcast.25, bf16[1024,128]{1,0:T(8,128)(2,1)S(1)} %copy-done.3, f32[512,1024]{1,0:T(8,128)S(1)} %feed.10.refs_4_, ...), custom_call_target="tpu_custom_call" | custom-call | flops 536870912 | bytes 8388608 | tf_op jit(solution)/shard_map/feed/pallas_call | solution.py:176
  93.1 2.1 %pad_maximum_fusion = bf16[2,2,2,4,9,64,128]{6,5,4,3,2,1,0:T(8,128)(2,1)S(1)} fusion(bf16[1,2,2,4,9,64,128]{6,5,4,3,2,1,0:T(8,128)(2,1)} %bitcast.14, bf16[1,2,2,4,9,64,128]{6,5,4,3,2,1,0:T(8,128)(2,1)S(1)} %bitcast.20), kind=kLoop, calls=%fused_computation | loop fusion | flops 2359296 | bytes 9437184 | tf_op jit(solution)/shard_map/stack | solution.py:306
  95.2 2.1 %score.1 = f32[4,8,128]{2,1,0:T(8,128)S(1)} custom-call(s32[4,8,4]{2,1,0:T(8,128)S(1)} %get-tuple-element.35.spots_ref, s32[4,8]{1,0:T(4,128)S(1)} %fusion.marks_ref, s32[4,8]{1,0:T(4,128)S(1)} %get-tuple-element.38.rows_ref, bf16[512,128]{1,0:T(8,128)(2,1)S(1)} %copy-done.2, bf16[288,64,128]{2,1,0:T(8,128)(2,1)S(1)} %bitcast.21), custom_call_target="tpu_custom_call" | custom-call | flops 268435456 | bytes 5242880 | tf_op jit(solution)/shard_map/score/pallas_call | solution.py:214
  (68 shorter events, 12.6 us)
Async XLA Ops:
  0.6 47.3 %collective-permute-start = (bf16[1024,1024]{1,0:T(8,128)(2,1)}, bf16[1024,1024]{1,0:T(8,128)(2,1)S(1)}, u32[]{:S(2)}, u32[]{:S(2)}) collective-permute-start(bf16[1024,1024]{1,0:T(8,128)(2,1)} %refs_1_.2), channel_id=1, source_target_pairs={{0,1},{1,0},{2,3},{3,2},{4,5},{5,4},{6,7},{7,6},{8,9},{9,8},{10,11... | collective-permute-start | bytes 6291464 | tf_op jit(solution)/shard_map/ppermute | solution.py:249
  1.1 46.8 %collective-permute-start.1 = (bf16[1024,1024]{1,0:T(8,128)(2,1)}, bf16[1024,1024]{1,0:T(8,128)(2,1)}, u32[]{:S(2)}, u32[]{:S(2)}) collective-permute-start(bf16[1024,1024]{1,0:T(8,128)(2,1)} %refs_2_.1), channel_id=1, source_target_pairs={{0,1},{1,0},{2,3},{3,2},{4,5},{5,4},{6,7},{7,6},{8,9},{9,8},{10,11... | collective-permute-start | bytes 6291464 | tf_op jit(solution)/shard_map/ppermute | solution.py:249
  2.9 7.2 %collective-permute-start.2 = (bf16[9,64,128]{2,1,0:T(8,128)(2,1)S(1)}, bf16[9,64,128]{2,1,0:T(8,128)(2,1)S(1)}, u32[]{:S(2)}, u32[]{:S(2)}) collective-permute-start(bf16[9,64,128]{2,1,0:T(8,128)(2,1)S(1)} %get-tuple-element.33), channel_id=1, source_target_pairs={{0,8},{4,12},{8,0},{12,4},{16,24},{20,28},{24,16},{28,20},{1,9},{5... | collective-permute-start | bytes 442376 | tf_op jit(solution)/shard_map/ppermute | solution.py:260
  7.0 5.9 %copy-start.10 = (bf16[512,1024]{1,0:T(8,128)(2,1)S(1)}, bf16[512,1024]{1,0:T(8,128)(2,1)}, u32[]{:S(2)}) copy-start(bf16[512,1024]{1,0:T(8,128)(2,1)} %tokens_ref.3) | copy-start | bytes 3145732
  8.3 32.2 %collective-permute-start.5 = (bf16[2,1024,256]{2,1,0:T(8,128)(2,1)S(1)}, bf16[2,1024,256]{2,1,0:T(8,128)(2,1)S(1)}, u32[]{:S(2)}, u32[]{:S(2)}) collective-permute-start(bf16[2,1024,256]{2,1,0:T(8,128)(2,1)S(1)} %pad_maximum_fusion.3), channel_id=1, source_target_pairs={{0,2},{1,3},{2,0},{3,1},{4,6},{5,7},{6,4},{7,5},{8,10},{9,11},{10,... | collective-permute-start | bytes 3145736 | tf_op jit(solution)/shard_map/ppermute | solution.py:252
  10.1 15.8 %collective-permute-start.3 = (bf16[2,9,64,128]{3,2,1,0:T(8,128)(2,1)S(1)}, bf16[2,9,64,128]{3,2,1,0:T(8,128)(2,1)S(1)}, u32[]{:S(2)}, u32[]{:S(2)}) collective-permute-start(bf16[2,9,64,128]{3,2,1,0:T(8,128)(2,1)S(1)} %get-tuple-element.31), channel_id=1, source_target_pairs={{0,16},{4,20},{8,24},{12,28},{16,0},{20,4},{24,8},{28,12},{1,17},{... | collective-permute-start | bytes 884744 | tf_op jit(solution)/shard_map/ppermute | solution.py:260
  26.0 14.4 %collective-permute-start.4 = (bf16[4,9,64,128]{3,2,1,0:T(8,128)(2,1)S(1)}, bf16[4,9,64,128]{3,2,1,0:T(8,128)(2,1)S(1)}, u32[]{:S(2)}, u32[]{:S(2)}) collective-permute-start(bf16[4,9,64,128]{3,2,1,0:T(8,128)(2,1)S(1)} %gate.4), channel_id=1, source_target_pairs={{0,4},{4,0},{8,12},{12,8},{16,20},{20,16},{24,28},{28,24},{1,5},{5... | collective-permute-start | bytes 1769480 | tf_op jit(solution)/shard_map/ppermute | solution.py:255
  40.4 4.7 %copy-start.5 = (bf16[1024,1024]{1,0:T(8,128)(2,1)S(1)}, bf16[1024,1024]{1,0:T(8,128)(2,1)}, u32[]{:S(2)}) copy-start(bf16[1024,1024]{1,0:T(8,128)(2,1)} %refs_2_.1) | copy-start | bytes 6291460
  40.5 4.5 %copy-start.4 = (bf16[1024,1024]{1,0:T(8,128)(2,1)S(1)}, bf16[1024,1024]{1,0:T(8,128)(2,1)}, u32[]{:S(2)}) copy-start(bf16[1024,1024]{1,0:T(8,128)(2,1)} %refs_1_.2) | copy-start | bytes 6291460
  40.5 23.3 %collective-permute-start.6 = (bf16[2,1024,256]{2,1,0:T(8,128)(2,1)S(1)}, bf16[2,1024,256]{2,1,0:T(8,128)(2,1)S(1)}, u32[]{:S(2)}, u32[]{:S(2)}) collective-permute-start(bf16[2,1024,256]{2,1,0:T(8,128)(2,1)S(1)} %get-tuple-element.22.refs_0_), channel_id=1, source_target_pairs={{0,4},{4,0},{8,12},{12,8},{16,20},{20,16},{24,28},{28,24},{1,5},{5... | collective-permute-start | bytes 3145736 | tf_op jit(solution)/shard_map/ppermute | solution.py:260
  41.8 24.0 %collective-permute-start.7 = (bf16[2,1024,256]{2,1,0:T(8,128)(2,1)S(1)}, bf16[2,1024,256]{2,1,0:T(8,128)(2,1)S(1)}, u32[]{:S(2)}, u32[]{:S(2)}) collective-permute-start(bf16[2,1024,256]{2,1,0:T(8,128)(2,1)S(1)} %get-tuple-element.22.refs_0_), channel_id=1, source_target_pairs={{0,8},{4,12},{8,0},{12,4},{16,24},{20,28},{24,16},{28,20},{1,9},{5... | collective-permute-start | bytes 3145736 | tf_op jit(solution)/shard_map/ppermute | solution.py:260
  43.5 26.5 %collective-permute-start.11 = (bf16[2,4,9,64,128]{4,3,2,1,0:T(8,128)(2,1)S(1)}, bf16[2,4,9,64,128]{4,3,2,1,0:T(8,128)(2,1)S(1)}, u32[]{:S(2)}, u32[]{:S(2)}) collective-permute-start(bf16[2,4,9,64,128]{4,3,2,1,0:T(8,128)(2,1)S(1)} %get-tuple-element.26), channel_id=1, source_target_pairs={{0,2},{1,3},{2,0},{3,1},{4,6},{5,7},{6,4},{7,5},{8,10},{9,11},{10,... | collective-permute-start | bytes 3538952 | tf_op jit(solution)/shard_map/ppermute | solution.py:252
  65.7 7.4 %collective-permute-start.8 = (bf16[2,1024,256]{2,1,0:T(8,128)(2,1)S(1)}, bf16[2,1024,256]{2,1,0:T(8,128)(2,1)S(1)}, u32[]{:S(2)}, u32[]{:S(2)}) collective-permute-start(bf16[2,1024,256]{2,1,0:T(8,128)(2,1)S(1)} %get-tuple-element.23.refs_2_), channel_id=1, source_target_pairs={{0,1},{1,0},{2,3},{3,2},{4,5},{5,4},{6,7},{7,6},{8,9},{9,8},{10,11... | collective-permute-start | bytes 3145736 | tf_op jit(solution)/shard_map/ppermute | solution.py:249
  65.7 7.4 %collective-permute-start.9 = (bf16[2,1024,256]{2,1,0:T(8,128)(2,1)S(1)}, bf16[2,1024,256]{2,1,0:T(8,128)(2,1)S(1)}, u32[]{:S(2)}, u32[]{:S(2)}) collective-permute-start(bf16[2,1024,256]{2,1,0:T(8,128)(2,1)S(1)} %get-tuple-element.24.refs_3_), channel_id=1, source_target_pairs={{0,1},{1,0},{2,3},{3,2},{4,5},{5,4},{6,7},{7,6},{8,9},{9,8},{10,11... | collective-permute-start | bytes 3145736 | tf_op jit(solution)/shard_map/ppermute | solution.py:249
  66.2 6.9 %collective-permute-start.10 = (bf16[2,1024,256]{2,1,0:T(8,128)(2,1)S(1)}, bf16[2,1024,256]{2,1,0:T(8,128)(2,1)S(1)}, u32[]{:S(2)}, u32[]{:S(2)}) collective-permute-start(bf16[2,1024,256]{2,1,0:T(8,128)(2,1)S(1)} %get-tuple-element.25.refs_4_), channel_id=1, source_target_pairs={{0,1},{1,0},{2,3},{3,2},{4,5},{5,4},{6,7},{7,6},{8,9},{9,8},{10,11... | collective-permute-start | bytes 3145736 | tf_op jit(solution)/shard_map/ppermute | solution.py:249
  66.3 14.5 %collective-permute-start.12 = (bf16[2,1024,128]{2,1,0:T(8,128)(2,1)S(1)}, bf16[2,1024,128]{2,1,0:T(8,128)(2,1)}, u32[]{:S(2)}, u32[]{:S(2)}) collective-permute-start(bf16[2,1024,128]{2,1,0:T(8,128)(2,1)S(1)} %slice.25), channel_id=1, source_target_pairs={{0,8},{4,12},{8,0},{12,4},{16,24},{20,28},{24,16},{28,20},{1,9},{5... | collective-permute-start | bytes 1572872 | tf_op jit(solution)/shard_map/ppermute | solution.py:260
  70.0 12.3 %collective-permute-start.13 = (bf16[2,1024,128]{2,1,0:T(8,128)(2,1)S(1)}, bf16[2,1024,128]{2,1,0:T(8,128)(2,1)}, u32[]{:S(2)}, u32[]{:S(2)}) collective-permute-start(bf16[2,1024,128]{2,1,0:T(8,128)(2,1)S(1)} %slice.26), channel_id=1, source_target_pairs={{0,4},{4,0},{8,12},{12,8},{16,20},{20,16},{24,28},{28,24},{1,5},{5... | collective-permute-start | bytes 1572872 | tf_op jit(solution)/shard_map/ppermute | solution.py:260
  75.4 6.9 %copy-start = (f32[512,1024]{1,0:T(8,128)}, f32[512,1024]{1,0:T(8,128)S(1)}, u32[]{:S(2)}) copy-start(f32[512,1024]{1,0:T(8,128)S(1)} %feed.9.refs_3_.refs_1_) | copy-start | bytes 6291460
  75.4 7.4 %copy-start.12 = (s32[4,8]{1,0:T(4,128)S(1)}, s32[4,8]{1,0:T(4,128)}, u32[]{:S(2)}) copy-start(s32[4,8]{1,0:T(4,128)} %param.25) | copy-start | bytes 388
  82.3 10.8 %collective-permute-start.16 = (bf16[2,2,4,9,64,128]{5,4,3,2,1,0:T(8,128)(2,1)S(1)}, bf16[2,2,4,9,64,128]{5,4,3,2,1,0:T(8,128)(2,1)}, u32[]{:S(2)}, u32[]{:S(2)}) collective-permute-start(bf16[2,2,4,9,64,128]{5,4,3,2,1,0:T(8,128)(2,1)S(1)} %get-tuple-element.29), channel_id=1, source_target_pairs={{0,1},{1,0},{2,3},{3,2},{4,5},{5,4},{6,7},{7,6},{8,9},{9,8},{10,11... | collective-permute-start | bytes 7077896 | tf_op jit(solution)/shard_map/ppermute | solution.py:249
  82.3 5.4 %collective-permute-start.14 = (bf16[2,1024,128]{2,1,0:T(8,128)(2,1)}, bf16[2,1024,128]{2,1,0:T(8,128)(2,1)}, u32[]{:S(2)}, u32[]{:S(2)}) collective-permute-start(bf16[2,1024,128]{2,1,0:T(8,128)(2,1)} %get-tuple-element.27.refs_2_), channel_id=1, source_target_pairs={{0,1},{1,0},{2,3},{3,2},{4,5},{5,4},{6,7},{7,6},{8,9},{9,8},{10,11... | collective-permute-start | bytes 1572872 | tf_op jit(solution)/shard_map/ppermute | solution.py:249
  82.8 5.5 %collective-permute-start.15 = (bf16[2,1024,128]{2,1,0:T(8,128)(2,1)}, bf16[2,1024,128]{2,1,0:T(8,128)(2,1)}, u32[]{:S(2)}, u32[]{:S(2)}) collective-permute-start(bf16[2,1024,128]{2,1,0:T(8,128)(2,1)} %get-tuple-element.28.refs_3_), channel_id=1, source_target_pairs={{0,1},{1,0},{2,3},{3,2},{4,5},{5,4},{6,7},{7,6},{8,9},{9,8},{10,11... | collective-permute-start | bytes 1572872 | tf_op jit(solution)/shard_map/ppermute | solution.py:249
  84.7 3.6 %copy-start.3 = (bf16[1024,128]{1,0:T(8,128)(2,1)S(1)}, bf16[1024,128]{1,0:T(8,128)(2,1)}, u32[]{:S(2)}) copy-start(bf16[1024,128]{1,0:T(8,128)(2,1)} %refs_3_.1) | copy-start | bytes 786436
  84.7 3.6 %copy-start.6 = (f32[1024]{0:T(1024)S(1)}, f32[1024]{0:T(1024)}, u32[]{:S(2)}) copy-start(f32[1024]{0:T(1024)} %param.20) | copy-start | bytes 12292
  (6 other events, 11.2 us)
